TPU v7x, 512 devices: a whole 4x8x8 slice. The times are simulated.
512 devices in a mesh: mem: 64 (over z, x, core), dec: 8 (over y).
Axes of the slice: x: 4, y: 8, z: 8, core: 2. Of those that a mesh axis runs over, the one named last changes fastest.
Arguments:
- question_states: bfloat16 [64, 8, 4096], P('mem', None, 'dec'), may hold values from -6 to 6
- passage_cache: bfloat16 [256, 64, 4096], P('mem', None, 'dec'), may hold values from -6 to 6
- norm_gain: float32 [4096], replicated, may hold values from 0.1 to 1.9
- enc_wq: bfloat16 [4096, 2048], P('mem', 'dec'), may hold values from -0.09375 to 0.09375
- enc_wk: bfloat16 [4096, 2048], P('mem', 'dec'), may hold values from -0.09375 to 0.09375
- enc_wv: bfloat16 [4096, 2048], P('mem', 'dec'), may hold values from -0.09375 to 0.09375
- enc_wo: bfloat16 [2048, 4096], P('dec', 'mem'), may hold values from -0.125 to 0.125
- dec_wk: bfloat16 [4096, 2048], P('dec'), may hold values from -0.09375 to 0.09375
- dec_wv: bfloat16 [4096, 2048], P('dec'), may hold values from -0.09375 to 0.09375
- dec_queries: bfloat16 [64, 8, 2048], P('mem', None, 'dec'), may hold values from -6 to 6
- passage_ids: int32 [64, 2], replicated, may hold values from 0 to 255, as said below
- location: int32 [256], replicated, may hold values from 0 to 255, as said below
- question_lengths: int32 [64], replicated, may hold values from 1 to 8
Outputs:
- decoder_context: bfloat16 [64, 8, 2048], P('mem', None, 'dec')
Inputs may be any that keep to these rules, and one draw needn't show every extreme that they name: `passage_ids`: the requests whose passage lies in cache rows s * 4 to (s + 1) * 4 - 1 number at most 3 for every s, and exactly 3 for some s; a question's passages need not differ. A permutation: passage p's states are row location[p] of passage_cache.
All inputs are finite; a program needn't handle non-finite values.
Results may differ from a plain program's by a relative error of at most 0.04.
Values may be sent and summed in bfloat16 or wider, within the bound.
A program may use at most 64 MiB of HBM per device.

v0:
```python
import jax
import jax.numpy as jnp
from jax import lax
from jax.sharding import PartitionSpec as P

HEAD_DIM = 64
CAP = 3


NORM_EPSILON = 1e-06


def body(
    question_states,
    passage_cache,
    norm_gain,
    enc_wq,
    enc_wk,
    enc_wv,
    enc_wo,
    dec_wk,
    dec_wv,
    dec_queries,
    passage_ids,
    location,
    question_lengths,
):
    mem_count = lax.axis_size("mem")
    mem_index = lax.axis_index("mem")
    pass_count = passage_ids.shape[1]
    request_total = mem_count * pass_count
    stored_count = passage_cache.shape[0]
    question_rows = question_states.shape[1]
    pair_rows = question_rows + passage_cache.shape[1]
    answer_rows = dec_queries.shape[1]
    heads_here = dec_queries.shape[2] // HEAD_DIM
    score_scale = HEAD_DIM ** (-0.5)
    cache_row = jnp.take(location, passage_ids.reshape(-1))
    owner_index = cache_row // stored_count
    cache_slot = cache_row % stored_count
    served = (owner_index == mem_index).astype(jnp.int32)
    served_rank = jnp.cumsum(served) - 1
    taken_mask = (served[None, :] == 1) & (served_rank[None, :] == jnp.arange(CAP)[:, None])
    filled = jnp.any(taken_mask, axis=1)
    request = jnp.sum(jnp.where(taken_mask, jnp.arange(request_total)[None, :], 0), axis=1)
    asking = request // pass_count
    pick_index = request % pass_count
    local_slot = jnp.sum(jnp.where(taken_mask, cache_slot[None, :], 0), axis=1)
    every_question, every_query = (
        lax.all_gather(question_states, "mem", axis=0, tiled=True),
        lax.all_gather(dec_queries, "mem", axis=0, tiled=True),
    )
    asked_states = every_question[asking]
    asked_queries = every_query[asking]
    asked_passages = passage_cache[local_slot]
    local_rows = jnp.concatenate([asked_states, asked_passages], axis=1)
    full_rows = lax.all_gather(local_rows, "dec", axis=2, tiled=True)
    model_width = full_rows.shape[2]
    squares = jnp.mean(jnp.square(full_rows.astype(jnp.float32)), axis=2, keepdims=True)
    normed = (full_rows.astype(jnp.float32) * lax.rsqrt(squares + NORM_EPSILON) * norm_gain).astype(
        jnp.bfloat16
    )
    row_total = CAP * pair_rows
    flattened = normed.reshape(row_total, model_width)
    local_width = enc_wq.shape[1]
    pieces = (
        lax.all_gather(enc_wq, "mem", axis=0, tiled=True),
        lax.all_gather(enc_wk, "mem", axis=0, tiled=True),
        lax.all_gather(enc_wv, "mem", axis=0, tiled=True),
    )
    query_sums, key_sums, value_sums = tuple(
        (
            jnp.dot(flattened, weight_piece, preferred_element_type=jnp.float32)
            for weight_piece in pieces
        )
    )
    shape_four = (CAP, pair_rows, heads_here, HEAD_DIM)
    queries = query_sums.astype(jnp.bfloat16).reshape(shape_four)
    enc_keys = key_sums.astype(jnp.bfloat16).reshape(shape_four)
    enc_values = value_sums.astype(jnp.bfloat16).reshape(shape_four)
    lengths_here = question_lengths[asking]
    positions = jnp.arange(pair_rows)
    live_keys = (
        (positions[None, :] >= question_rows) | (positions[None, :] < lengths_here[:, None])
    ).astype(jnp.float32)
    scores = (
        jnp.einsum("cihe,cjhe->chij", queries, enc_keys, preferred_element_type=jnp.float32)
        * score_scale
    )
    weights = jnp.exp(scores) * live_keys[:, None, None, :]
    probabilities = (weights / jnp.sum(weights, axis=3, keepdims=True)).astype(jnp.bfloat16)
    context = (
        jnp.einsum("chij,cjhe->cihe", probabilities, enc_values, preferred_element_type=jnp.float32)
        .astype(jnp.bfloat16)
        .reshape(row_total, local_width)
    )
    partial_out = jnp.dot(
        context,
        lax.all_gather(enc_wo, "mem", axis=1, tiled=True),
        preferred_element_type=jnp.float32,
    )
    attended = lax.psum_scatter(
        partial_out.astype(jnp.bfloat16), "dec", scatter_dimension=1, tiled=True
    ).astype(jnp.float32)
    encoded = (local_rows.reshape(row_total, -1).astype(jnp.float32) + attended).astype(
        jnp.bfloat16
    )
    key_part = jnp.dot(encoded, dec_wk, preferred_element_type=jnp.float32)
    value_part = jnp.dot(encoded, dec_wv, preferred_element_type=jnp.float32)
    key_share, value_share = (
        lax.psum_scatter(
            key_part.astype(jnp.bfloat16), "dec", scatter_dimension=1, tiled=True
        ).astype(jnp.float32),
        lax.psum_scatter(
            value_part.astype(jnp.bfloat16), "dec", scatter_dimension=1, tiled=True
        ).astype(jnp.float32),
    )
    dec_keys = key_share.astype(jnp.bfloat16).reshape(shape_four)
    dec_values = value_share.astype(jnp.bfloat16).reshape(shape_four)
    asked = asked_queries.reshape(CAP, answer_rows, heads_here, HEAD_DIM)
    cross_scores = (
        jnp.einsum("cahe,cjhe->chaj", asked, dec_keys, preferred_element_type=jnp.float32)
        * score_scale
    )
    keep_keys = live_keys * filled.astype(jnp.float32)[:, None]
    cross_weight = jnp.exp(cross_scores) * keep_keys[:, None, None, :]
    numerators = jnp.einsum(
        "chaj,cjhe->cahe",
        cross_weight.astype(jnp.bfloat16),
        dec_values,
        preferred_element_type=jnp.float32,
    ).reshape(CAP, -1)
    denominators = jnp.transpose(jnp.sum(cross_weight, axis=3), (0, 2, 1)).reshape(CAP, -1)
    target_pairs = (
        (asking[:, None, None] == jnp.arange(mem_count)[None, :, None])
        & (pick_index[:, None, None] == jnp.arange(pass_count)[None, None, :])
        & filled[:, None, None]
    ).astype(jnp.float32)
    back_numer = jnp.einsum(
        "cqk,cx->qkx", target_pairs, numerators, precision=lax.Precision.HIGHEST
    )
    back_denom = jnp.einsum(
        "cqk,cx->qkx", target_pairs, denominators, precision=lax.Precision.HIGHEST
    )
    got_numer, got_denom = (
        lax.all_to_all(
            back_numer.astype(jnp.bfloat16), "mem", split_axis=0, concat_axis=0, tiled=True
        ).astype(back_numer.dtype),
        lax.all_to_all(
            back_denom.astype(jnp.bfloat16), "mem", split_axis=0, concat_axis=0, tiled=True
        ).astype(back_denom.dtype),
    )
    numerator_sum = jnp.sum(got_numer, axis=(0, 1))
    denominator_sum = jnp.sum(got_denom, axis=(0, 1))
    answer = (
        numerator_sum.reshape(answer_rows, heads_here, HEAD_DIM)
        / denominator_sum.reshape(answer_rows, heads_here)[:, :, None]
    )
    return answer.reshape(1, answer_rows, heads_here * HEAD_DIM).astype(jnp.bfloat16)


def solution(mesh):
    in_specs = (
        P("mem", None, "dec"),
        P("mem", None, "dec"),
        P(),
        P("mem", "dec"),
        P("mem", "dec"),
        P("mem", "dec"),
        P("dec", "mem"),
        P("dec", None),
        P("dec", None),
        P("mem", None, "dec"),
        P(),
        P(),
        P(),
    )
    out_specs = P("mem", None, "dec")
    return jax.shard_map(body, mesh=mesh, in_specs=in_specs, out_specs=out_specs, check_vma=False)
```

profile of v0, /device:TPU:1, one launch (start us, length us, event | category | flops | bytes accessed | tf_op | source)
XLA Modules:
  0.0 616.9 jit_solution(16126858956598190746)
XLA Ops:
  7.8 1.6 gather_fusion
  10.3 57.7 %all_gather.21 = bf16[64,8,512]{2,1,0:T(8,128)(2,1)S(1)} all-gather(bf16[1,8,512]{2,1,0:T(8,128)(2,1)} %param.13), channel_id=1, replica_groups=mesh['mem'=64,'dec'=8] {'mem'}, dimensions={0}, use_global_device_ids=true | all-gather | bytes 532480 | tf_op jit(solution)/shard_map/all_gather | solution.py:50
  68.5 1.5 gather_fusion.2
  74.2 32.3 %all-gather.6.cloned.1.call-done = bf16[3,72,4096]{2,1,0:T(8,128)(2,1)} async-done(((bf16[3,72,512]{2,1,0:T(8,128)(2,1)}), bf16[3,72,4096]{2,1,0:T(8,128)(2,1)}) %all-gather.6.cloned.1.call-update) | async-done | bytes 1769488 | tf_op jit(solution)/shard_map/all_gather | solution.py:57
  106.5 2.1 fusion
  108.6 1.8 fusion.2
  110.4 85.7 %all-gather.10.cloned.1.call-done = bf16[4096,256]{1,0:T(8,128)(2,1)} async-done(((bf16[64,256]{1,0:T(8,128)(2,1)}), bf16[4096,256]{1,0:T(8,128)(2,1)}) %all-gather.10.cloned.1.call-update) | async-done | bytes 2097168 | tf_op jit(solution)/shard_map/all_gather | solution.py:67
  196.1 2.8 convolution_convert_fusion.6
  199.1 81.1 %all-gather.12.cloned.1.call-done = bf16[4096,256]{1,0:T(8,128)(2,1)} async-done(((bf16[64,256]{1,0:T(8,128)(2,1)}), bf16[4096,256]{1,0:T(8,128)(2,1)}) %all-gather.12.cloned.1.call-update) | async-done | bytes 2097168 | tf_op jit(solution)/shard_map/all_gather | solution.py:68
  280.1 2.8 convolution_convert_fusion.5
  283.0 80.9 %all-gather.8.cloned.1.call-done = bf16[4096,256]{1,0:T(8,128)(2,1)} async-done(((bf16[64,256]{1,0:T(8,128)(2,1)}), bf16[4096,256]{1,0:T(8,128)(2,1)}) %all-gather.8.cloned.1.call-update) | async-done | bytes 2097168 | tf_op jit(solution)/shard_map/all_gather | solution.py:69
  363.9 2.8 convolution_convert_fusion.7
  367.8 79.9 %all-gather.14.cloned.1.call-done = bf16[256,4096]{0,1:T(8,128)(2,1)} async-done(((bf16[256,64]{0,1:T(8,128)(2,1)}), bf16[256,4096]{0,1:T(8,128)(2,1)}) %all-gather.14.cloned.1.call-update) | async-done | bytes 2097168 | tf_op jit(solution)/shard_map/all_gather | solution.py:99
  447.8 3.6 convolution_convert_fusion
  451.5 36.2 %reduce-scatter.4.cloned.1.call-done = bf16[216,512]{1,0:T(8,128)(2,1)} async-done(((bf16[216,4096]{1,0:T(8,128)(2,1)}), bf16[216,512]{1,0:T(8,128)(2,1)}) %reduce-scatter.4.cloned.1.call-update) | async-done | bytes 221200 | tf_op jit(solution)/shard_map/reduce_scatter | solution.py:102
  488.6 1.6 convolution_convert_fusion.1
  490.3 3.2 convolution_convert_fusion.2
  493.5 50.4 %all_gather.27 = bf16[64,8,256]{2,1,0:T(8,128)(2,1)S(1)} all-gather(bf16[1,8,256]{2,1,0:T(8,128)(2,1)S(1)} %copy-done.6), channel_id=1, replica_groups=mesh['mem'=64,'dec'=8] {'mem'}, dimensions={0}, use_global_device_ids=true | all-gather | bytes 266240 | tf_op jit(solution)/shard_map/all_gather | solution.py:51
  544.7 1.1 reshape.512
  547.2 7.2 %all-to-all-start.1 = ((bf16[64,2,32]{2,1,0:T(2,128)(2,1)}), bf16[64,2,32]{2,1,0:T(2,128)(2,1)S(1)}, u32[]{:S(2)}, u32[]{:S(2)}) async-start(bf16[64,2,32]{2,1,0:T(2,128)(2,1)} %copy.77), calls=%async_computation.4 | async-start | bytes 65536 | tf_op jit(solution)/shard_map/all_to_all | solution.py:149
  554.4 18.4 %reduce-scatter.6.cloned.1.call-done = bf16[216,256]{1,0:T(8,128)(2,1)} async-done(((bf16[216,2048]{1,0:T(8,128)(2,1)}), bf16[216,256]{1,0:T(8,128)(2,1)}) %reduce-scatter.6.cloned.1.call-update) | async-done | bytes 110608 | tf_op jit(solution)/shard_map/reduce_scatter | solution.py:114
  574.9 1.3 copy.75
  576.2 15.1 %all-to-all-start = ((bf16[64,2,2048]{2,1,0:T(2,128)(2,1)}), bf16[64,2,2048]{2,1,0:T(2,128)(2,1)S(1)}, u32[]{:S(2)}, u32[]{:S(2)}) async-start(bf16[64,2,2048]{2,1,0:T(2,128)(2,1)} %copy.75), calls=%async_computation.3 | async-start | bytes 1048576 | tf_op jit(solution)/shard_map/all_to_all | solution.py:146
  591.6 17.4 %all-to-all-done = bf16[64,2,2048]{2,1,0:T(2,128)(2,1)S(1)} async-done(((bf16[64,2,2048]{2,1,0:T(2,128)(2,1)}), bf16[64,2,2048]{2,1,0:T(2,128)(2,1)S(1)}, u32[]{:S(2)}, u32[]{:S(2)}) %all-to-all-start) | async-done | bytes 524320 | tf_op jit(solution)/shard_map/all_to_all | solution.py:146
  (88 shorter events, 14.8 us)
Async XLA Ops:
  6.5 482.1 %copy-start = (bf16[512,2048]{1,0:T(8,128)(2,1)S(1)}, bf16[512,2048]{1,0:T(8,128)(2,1)}, u32[]{:S(2)}) copy-start(bf16[512,2048]{1,0:T(8,128)(2,1)} %param.20) | copy-start | bytes 6291460
  6.5 66.9 %copy-start.1 = (s32[64]{0:T(128)S(1)}, s32[64]{0:T(128)}, u32[]{:S(2)}) copy-start(s32[64]{0:T(128)} %param.25) | copy-start | bytes 772
  6.5 100.0 %all-gather.6.cloned.1.call-start = ((), (), s32[]{:S(2)}) async-start(), calls=%async_computation.5 | async-start | bytes 1990656 | tf_op jit(solution)/shard_map/all_gather | solution.py:57
  9.8 98.8 %copy-start.5 = (f32[4096]{0:T(1024)S(1)}, f32[4096]{0:T(1024)}, u32[]{:S(2)}) copy-start(f32[4096]{0:T(1024)} %param.15) | copy-start | bytes 49156
  70.1 0.7 copy-start.3
  70.8 125.3 %all-gather.10.cloned.1.call-start = ((), (), s32[]{:S(2)}) async-start(), calls=%async_computation.7 | async-start | bytes 2129920 | tf_op jit(solution)/shard_map/all_gather | solution.py:67
  71.5 208.6 %all-gather.12.cloned.1.call-start = ((), (), s32[]{:S(2)}) async-start(), calls=%async_computation.8 | async-start | bytes 2129920 | tf_op jit(solution)/shard_map/all_gather | solution.py:68
  72.3 291.7 %all-gather.8.cloned.1.call-start = ((), (), s32[]{:S(2)}) async-start(), calls=%async_computation.6 | async-start | bytes 2129920 | tf_op jit(solution)/shard_map/all_gather | solution.py:69
  72.8 374.9 %all-gather.14.cloned.1.call-start = ((), (), s32[]{:S(2)}) async-start(), calls=%async_computation.9 | async-start | bytes 2129920 | tf_op jit(solution)/shard_map/all_gather | solution.py:99
  73.4 414.2 %reduce-scatter.4.cloned.1.call-start = ((), (), s32[]{:S(2)}) async-start(), calls=%async_computation.10 | async-start | bytes 1990656 | tf_op jit(solution)/shard_map/reduce_scatter | solution.py:102
  106.5 2.1 copy-start.2
  367.8 119.8 %copy-start.4 = (bf16[3,72,512]{2,1,0:T(8,128)(2,1)S(1)}, bf16[3,72,512]{2,1,0:T(8,128)(2,1)}, u32[]{:S(2)}) copy-start(bf16[3,72,512]{2,1,0:T(8,128)(2,1)} %copy-done.3) | copy-start | bytes 663556
  451.4 93.3 %reduce-scatter.8.cloned.1.call-start = ((), (), s32[]{:S(2)}) async-start(), calls=%async_computation.12 | async-start | bytes 995328 | tf_op jit(solution)/shard_map/reduce_scatter | solution.py:111
  490.2 3.3 copy-start.6
  490.3 82.6 %reduce-scatter.6.cloned.1.call-start = ((), (), s32[]{:S(2)}) async-start(), calls=%async_computation.11 | async-start | bytes 995328 | tf_op jit(solution)/shard_map/reduce_scatter | solution.py:114
  547.2 29.0 %all-to-all-start.1 = ((bf16[64,2,32]{2,1,0:T(2,128)(2,1)}), bf16[64,2,32]{2,1,0:T(2,128)(2,1)S(1)}, u32[]{:S(2)}, u32[]{:S(2)}) async-start(bf16[64,2,32]{2,1,0:T(2,128)(2,1)} %copy.77), calls=%async_computation.4 | async-start | bytes 65536 | tf_op jit(solution)/shard_map/all_to_all | solution.py:149
  576.2 32.8 %all-to-all-start = ((bf16[64,2,2048]{2,1,0:T(2,128)(2,1)}), bf16[64,2,2048]{2,1,0:T(2,128)(2,1)S(1)}, u32[]{:S(2)}, u32[]{:S(2)}) async-start(bf16[64,2,2048]{2,1,0:T(2,128)(2,1)} %copy.75), calls=%async_computation.3 | async-start | bytes 1048576 | tf_op jit(solution)/shard_map/all_to_all | solution.py:146
Sparse Core Ops, SparseCore 0:
  70.9 35.5 all-gather.5
  109.9 86.2 all-gather.9
  199.5 80.5 all-gather.11
  283.3 80.5 all-gather.7
  367.1 80.5 all-gather.13
  451.5 36.0 reduce-scatter.3
  490.5 38.9 reduce-scatter.7
  532.5 40.2 reduce-scatter.5
where the time goes:
time: 617 us
  waiting for transfers between devices  434 us (70%)
  blocking collectives  108 us (18%)
  starting transfers between devices  22.5 us (4%)
  matrix products  18.6 us (3%)
  between operations  13.8 us (2%)
  local copies, waits for them, and re-layouts  12.4 us (2%)
  other arithmetic  7.01 us (1%)
    all_gather x1, waiting for transfers between devices, body(): lax.all_gather(enc_wq, 'mem', axis=0, tiled=True)  85.7 us
    all_gather x1, waiting for transfers between devices, body(): lax.all_gather(enc_wk, 'mem', axis=0, tiled=True)  81.1 us
    all_gather x1, waiting for transfers between devices, body(): lax.all_gather(enc_wv, 'mem', axis=0, tiled=True)  80.9 us
    all_gather x1, waiting for transfers between devices, body(): lax.all_gather(enc_wo, 'mem', axis=1, tiled=True)  79.9 us
    all_gather x1, blocking collectives, body(): lax.all_gather(question_states, 'mem', axis=0, tiled=True)  57.7 us
    all_gather x1, blocking collectives, body(): lax.all_gather(dec_queries, 'mem', axis=0, tiled=True)  50.4 us
    reduce_scatter x1, waiting for transfers between devices, body(): lax.psum_scatter(partial_out.astype(jnp.bfloat16), 'dec', scatter_dimensi...  36.2 us
    all_gather x1, waiting for transfers between devices, body(): full_rows = lax.all_gather(local_rows, 'dec', axis=2, tiled=True)  32.3 us
  transfers between devices with their start and end apart: 10, of which 8 were waited for; matrix products, arithmetic and copies ran while one was open for 4% of the time, Pallas kernels for 0%

commit v1 on v0

v1 whole, which is shorter than its diff:
```python
import functools

import jax
import jax.numpy as jnp
from jax import lax
from jax.experimental import pallas as pl
from jax.experimental.pallas import tpu as pltpu
from jax.sharding import PartitionSpec as P

MESH = pl.DeviceIdType.MESH
BF16, F32 = jnp.bfloat16, jnp.float32
ZN, XN, YN = 8, 4, 8
CAP = 3
HEAD_DIM = 64
NORM_EPSILON = 1e-06
FAR_FIRST = (4, 3, 5, 2, 6, 1, 7)
NT = (((1,), (1,)), ((), ()))


def wrap(value, size):
    return lax.rem(value + size, size)


def dot_nt(a, b):
    return lax.dot_general(a, b, NT, preferred_element_type=F32)


def kernel(
    meta, qs, cache, gain, wq, wk, wv, wo, dwk_hbm, dwv_hbm, dq,
    out,
    wg, wot, wot_own, xg, qg, dqg, xn, ctxg, enc, ekeys, dqp, cs, cr, cwg, ns, nr, t1s, t1r, t2s, t2r, dwk, dwv,
    load_sem, ring_send, ring1, ring2, sib_recv, yx_send, yx_recv,
    qz_s, qz_r, qx_s, qx_r, qs_s, qs_r, qy_s, qy_r,
    wp_s, wp_r, wz_s, wz_r, wx_s, wx_r, ws_s, ws_r,
    cx_s, cx_r, a_s, a_r, b_s, b_r, n_s, n_r, f_s, f_r, h_s, h_r,
):
    m = lax.axis_index("mem")
    y = lax.axis_index("dec")
    z = m // (2 * XN)
    x = lax.rem(m // 2, XN)
    core = lax.rem(m, 2)
    r8 = lax.rem(m, 8)

    def device(zz, xx, cc, yy):
        return ((zz * XN + xx) * 2 + cc, yy)

    def at_z(k):
        return device(wrap(z + k, ZN), x, core, y)

    def at_x(k):
        return device(z, wrap(x + k, XN), core, y)

    def at_y(k):
        return device(z, x, core, wrap(y + k, YN))

    def at_xc(k):
        other = lax.rem(r8 + k, 8)
        return (z * 8 + other, y)

    sibling = device(z, x, 1 - core, y)
    swap = (8 * y + r8, z)
    has_swap = z != y

    def remote(src, dst, send, recv, to):
        return pltpu.make_async_remote_copy(
            src_ref=src, dst_ref=dst, send_sem=send, recv_sem=recv, device_id=to, device_id_type=MESH
        )

    barrier = pltpu.get_barrier_semaphore()
    for k in range(1, 8):
        pl.semaphore_signal(barrier, inc=1, device_id=at_y(k), device_id_type=MESH)
        pl.semaphore_signal(barrier, inc=1, device_id=at_z(k), device_id_type=MESH)
        pl.semaphore_signal(barrier, inc=1, device_id=at_xc(k), device_id_type=MESH)

    @pl.when(has_swap)
    def _():
        pl.semaphore_signal(barrier, inc=1, device_id=swap, device_id_type=MESH)

    load_k = pltpu.make_async_copy(dwk_hbm, dwk, load_sem.at[0])
    load_v = pltpu.make_async_copy(dwv_hbm, dwv, load_sem.at[1])
    load_k.start()
    load_v.start()

    first = qs[0].astype(F32)
    second = jnp.concatenate([first[:, 384:512], dq[0].astype(F32)], axis=1)
    own_q = (core * XN + x) * ZN + z
    qg[own_q] = jnp.concatenate([first[:, 0:384], second], axis=0).astype(BF16)
    wg[m] = jnp.concatenate([wq[...], wk[...], wv[...]], axis=1)
    turned = jnp.transpose(wo[...].astype(F32)).astype(BF16)
    wot_own[...] = turned
    own_w = (core * XN + x) * ZN + z

    @pl.when(jnp.logical_not(has_swap))
    def _():
        wot[own_w] = wot_own[...]

    for c in range(CAP):
        xg[y, 64 * c : 64 * c + 64, :] = cache[meta[c]]

    @pl.when(has_swap)
    def _():
        pl.semaphore_wait(barrier, 22)

    @pl.when(jnp.logical_not(has_swap))
    def _():
        pl.semaphore_wait(barrier, 21)

    def q_z(k, source):
        sl = qg.at[(core * XN + x) * ZN + wrap(source, ZN)]
        return remote(sl, sl, qz_s.at[k], qz_r.at[k], at_z(k))

    def q_x(k, source):
        sl = qg.at[pl.ds((core * XN + wrap(source, XN)) * ZN, ZN)]
        return remote(sl, sl, qx_s.at[k], qx_r.at[k], at_x(k))

    def q_s(cc):
        sl = qg.at[pl.ds(cc * (XN * ZN), XN * ZN)]
        return remote(sl, sl, qs_s.at[0], qs_r.at[0], sibling)

    def q_y(k, source):
        sl = xg.at[wrap(source, YN), pl.ds(192, 32)]
        sd = dqg.at[wrap(source, YN)]
        return (
            remote(sl, sl, qy_s.at[0, k], qy_r.at[0, k], at_y(k)),
            remote(sd, sd, qy_s.at[1, k], qy_r.at[1, k], at_y(k)),
        )

    def question_0():
        for k in FAR_FIRST:
            q_z(k, z).start()

    def question_1():
        for k in FAR_FIRST:
            q_z(k, z - k).wait_recv()
        for k in (2, 1, 3):
            q_x(k, x).start()

    def question_2():
        for k in (1, 2, 3):
            q_x(k, x - k).wait_recv()
        q_s(core).start()

    def question_3():
        q_s(1 - core).wait_recv()
        rows, queries = [], []
        for c in range(CAP):
            asked = qg[meta[4 + c]].astype(F32)
            rows.append(jnp.concatenate([asked[0:8], asked[8:16, 0:128]], axis=1))
            queries.append(asked[8:16, 128:384])
        rows.append(jnp.zeros((8, 512), F32))
        queries.append(jnp.zeros((8, 256), F32))
        xg[y, 192:224, :] = jnp.concatenate(rows, axis=0).astype(BF16)
        dqg[y] = jnp.concatenate(queries, axis=0).astype(BF16)
        for k in FAR_FIRST:
            for copy in q_y(k, y):
                copy.start()

    def question_end():
        for k in FAR_FIRST:
            for copy in q_y(k, y - k):
                copy.wait_recv()

    def w_swap():
        return remote(wot_own, wot.at[(lax.rem(r8, 2) * XN + r8 // 2) * ZN + y], wp_s.at[0], wp_r.at[0], swap)

    def w_z(k, source):
        sl = wot.at[(core * XN + x) * ZN + wrap(source, ZN)]
        return remote(sl, sl, wz_s.at[k], wz_r.at[k], at_z(k))

    def w_x(k, source):
        sl = wot.at[pl.ds((core * XN + wrap(source, XN)) * ZN, ZN)]
        return remote(sl, sl, wx_s.at[k], wx_r.at[k], at_x(k))

    def w_s(cc):
        sl = wot.at[pl.ds(cc * (XN * ZN), XN * ZN)]
        return remote(sl, sl, ws_s.at[0], ws_r.at[0], sibling)

    def wout_0():
        @pl.when(has_swap)
        def _():
            w_swap().start()

    def wout_1():
        @pl.when(has_swap)
        def _():
            w_swap().wait_recv()

        for k in FAR_FIRST:
            w_z(k, z).start()

    def wout_2():
        for k in FAR_FIRST:
            w_z(k, z - k).wait_recv()
        for k in (2, 1, 3):
            w_x(k, x).start()

    def wout_3():
        for k in (1, 2, 3):
            w_x(k, x - k).wait_recv()
        w_s(core).start()

    def y_copy(c, sign, step, source):
        if step < YN // 2:
            sl = xg.at[wrap(source, YN), pl.ds(64 * c, 64)]
        else:
            sl = xg.at[wrap(source, YN), pl.ds(64 * c + (0 if sign > 0 else 32), 32)]
        d = 0 if sign > 0 else 1
        return remote(sl, sl, yx_send.at[c, d, step], yx_recv.at[c, d, step], at_y(sign))

    def rows_step(step):
        for c in range(CAP):
            for sign in (1, -1):
                if step > 0:
                    y_copy(c, sign, step, y - sign * step).wait_recv()
                if step < YN // 2:
                    y_copy(c, sign, step + 1, y - sign * step).start()

    def weights(role):
        n1, n2 = (ZN, XN) if role == 0 else (XN, ZN)
        i1, i2 = (z, x) if role == 0 else (x, z)
        sends = []

        def near(dim, sign):
            along_z = (dim == 1) == (role == 0)
            return at_z(sign) if along_z else at_x(sign)

        def chip(o, p):
            a, b = wrap(i1 + o, n1), wrap(i2 + p, n2)
            return a * XN + b if role == 0 else b * XN + a

        def view(o, p, half):
            index = chip(o, p) * 2 + role
            return wg.at[index] if half is None else wg.at[index, pl.ds(32 * half, 32)]

        def copy(o, p, half, recv, to, number):
            sl = view(o, p, half)
            return remote(sl, sl, ring_send.at[number], recv, to)

        def start(o, p, half, recv, to):
            copy(o, p, half, recv, to, len(sends)).start()
            sends.append(half)

        def hand_over(o, p):
            start(o, p, None, sib_recv.at[chip(o, p)], sibling)

        def half_of(sign):
            return 0 if sign > 0 else 1

        def pass_on(dim, o, p, sign, step):
            count = n1 if dim == 1 else n2
            half = half_of(sign) if step == count // 2 else None
            recv = ring1.at[half_of(sign), step] if dim == 1 else ring2.at[o % n1, half_of(sign), step]
            start(o, p, half, recv, near(dim, sign))

        def arrived(dim, o, p, sign, step):
            count = n1 if dim == 1 else n2
            half = half_of(sign) if step == count // 2 else None
            recv = ring1.at[half_of(sign), step] if dim == 1 else ring2.at[o % n1, half_of(sign), step]
            copy(o, p, half, recv, near(dim, sign), 0).wait_recv()

        def second(o):
            for sign in (1, -1):
                pass_on(2, o, 0, sign, 1)
            hand_over(o, 0)

        def arrive_1(step):
            for sign in (1, -1):
                arrived(1, -sign * step, 0, sign, step)
                if step < n1 // 2:
                    pass_on(1, -sign * step, 0, sign, step + 1)
                    second(-sign * step)
            if step == n1 // 2:
                second(step)

        def arrive_2(o, step):
            for sign in (1, -1):
                arrived(2, o, -sign * step, sign, step)
                if step < n2 // 2:
                    pass_on(2, o, -sign * step, sign, step + 1)
                    hand_over(o, -sign * step)
            if step == n2 // 2:
                hand_over(o, step)

        for time in range(n1 // 2 + n2 // 2 + 1):
            if time == 0:
                question_0()
                wout_0()
                for sign in (1, -1):
                    pass_on(1, 0, 0, sign, 1)
                second(0)
            elif time <= n1 // 2:
                arrive_1(time)
            if time <= YN // 2:
                rows_step(time)
            for step in range(1, n2 // 2 + 1):
                o = time - step
                if 0 <= o <= n1 // 2:
                    for signed in (o,) if o in (0, n1 // 2) else (o, -o):
                        arrive_2(signed, step)
            if time == 1:
                question_1()
            if time == 2:
                question_2()
            if time == 3:
                question_3()
            if time == 4:
                wout_1()
        return sends

    sends = [None, None]
    for role in (0, 1):

        @pl.when(core == role)
        def _():
            sends[role] = weights(role)

    for chip in range(ZN * XN):
        sl = wg.at[chip * 2 + (1 - core)]
        remote(sl, sl, ring_send.at[0], sib_recv.at[chip], sibling).wait_recv()
    question_end()
    wout_2()

    squares = jnp.zeros((224, 128), F32)
    for d in range(YN):
        block = xg[d].astype(F32)
        block = block * block
        squares += block[:, 0:128] + block[:, 128:256] + block[:, 256:384] + block[:, 384:512]
    inverse = lax.rsqrt(jnp.sum(squares, axis=1, keepdims=True) * (1.0 / (512 * YN)) + NORM_EPSILON)
    for d in range(YN):
        xn[:, 512 * d : 512 * d + 512] = (xg[d].astype(F32) * inverse * gain[d : d + 1, :]).astype(BF16)
    totals = []
    for part in range(3):
        weight = wg[:, :, 256 * part : 256 * part + 256].reshape(4096, 256)
        totals.append(jnp.dot(xn[...], weight, preferred_element_type=F32).astype(BF16))
    queries, keys, values = totals

    def pair_of(index):
        return jnp.where(index < 192, index // 64, jnp.minimum((index - 192) // 8, CAP - 1))

    row_ids = lax.broadcasted_iota(jnp.int32, (224, 224), 0)
    col_ids = lax.broadcasted_iota(jnp.int32, (224, 224), 1)
    col_pair = pair_of(col_ids)
    length = jnp.where(col_pair == 0, meta[8], jnp.where(col_pair == 1, meta[9], meta[10]))
    token = col_ids - 192 - 8 * col_pair
    live = (pair_of(row_ids) == col_pair) & (token < length)

    def ctx_copy(part, k, source, half):
        if half is None:
            sl = ctxg.at[wrap(source, YN), part]
        else:
            sl = ctxg.at[wrap(source, YN), part, pl.ds(112 * half, 112)]
        return sl

    def ctx_near(part, k):
        sl = ctx_copy(part, k, y, None)
        return remote(sl, sl, cx_s.at[part, k], cx_r.at[part, k], at_y(k - 3))

    for part in range(2):
        outs = []
        for h in (2 * part, 2 * part + 1):
            sl = slice(64 * h, 64 * h + 64)
            scores = dot_nt(queries[:, sl], keys[:, sl]) * (HEAD_DIM**-0.5)
            weight = jnp.where(live, jnp.exp(scores), 0.0)
            prob = (weight / jnp.sum(weight, axis=1, keepdims=True)).astype(BF16)
            outs.append(jnp.dot(prob, values[:, sl], preferred_element_type=F32))
        ctxg[y, part] = jnp.concatenate(outs, axis=1).astype(BF16)
        for k in (-2, 2, -1, 1):
            ctx_near(part, k + 3).start()

    def ctx_recv(part, k, half=None):
        sl = ctx_copy(part, k, y - k, half)
        return sl

    def ctx_wait(part, k, half=None):
        sl = ctx_recv(part, k, half)
        slot = k + 3 if abs(k) <= 2 else {3: 6, -3: 7, 4: 8, -4: 9}[k]
        remote(sl, sl, cx_s.at[part, 0], cx_r.at[part, slot], at_y(1)).wait_recv()

    def ctx_forward(part, sign):
        sl = ctx_copy(part, 0, y - 2 * sign, None)
        slot = 6 if sign > 0 else 7
        remote(sl, sl, cx_s.at[part, slot], cx_r.at[part, slot], at_y(sign)).start()
        half = 0 if sign > 0 else 1
        sl = ctx_copy(part, 0, y - 2 * sign, half)
        slot = 8 if sign > 0 else 9
        remote(sl, sl, cx_s.at[part, slot], cx_r.at[part, slot], at_y(2 * sign)).start()

    load_k.wait()
    lane_head = lax.broadcasted_iota(jnp.int32, (8, 256), 1) // 64
    for g in range(YN):
        asked = dqg[g].astype(F32)
        blocks = []
        for c in range(CAP):
            for h in range(4):
                blocks.append(jnp.where(lane_head == h, asked[8 * c : 8 * c + 8], 0.0))
        spread = jnp.concatenate(blocks, axis=0).astype(BF16)
        product = dot_nt(spread, dwk[:, 256 * g : 256 * g + 256]).astype(BF16)
        for c in range(CAP):
            dqp[c, 32 * g : 32 * g + 32, :] = product[32 * c : 32 * c + 32]

    for part in range(2):
        for sign in (1, -1):
            ctx_wait(part, 2 * sign)
            ctx_forward(part, sign)
    wout_3()
    for part in range(2):
        for sign in (1, -1):
            ctx_wait(part, sign)
            ctx_wait(part, 3 * sign)
            ctx_wait(part, 4 * sign, 0 if sign > 0 else 1)
    w_s(1 - core).wait_recv()

    attended = jnp.zeros((224, 512), F32)
    for d in range(YN):
        context = jnp.concatenate([ctxg[d, 0], ctxg[d, 1]], axis=1)
        weight = jnp.concatenate(
            [wot[((r % 2) * XN + r // 2) * ZN + d] for r in range(8)], axis=0
        )
        attended += dot_nt(context, weight)
    enc[...] = (xg[y].astype(F32) + attended).astype(BF16)

    for c in range(CAP):
        ekeys[c, 0:64, :] = enc[64 * c : 64 * c + 64, :]
        ekeys[c, 64:96, :] = enc[192:224, :]
        ekeys[c, 96:128, :] = jnp.zeros((32, 512), BF16)
        part = dot_nt(dqp[c], ekeys[c]).astype(BF16)
        for g in range(YN):
            cs[g, 32 * c : 32 * c + 32, :] = part[32 * g : 32 * g + 32]

    def scatter(src, dst, send, recv, k):
        return remote(src.at[wrap(y + k, YN)], dst.at[y], send.at[k], recv.at[k], at_y(k))

    def scattered(src, dst, send, recv, k):
        sl = dst.at[wrap(y - k, YN)]
        return remote(sl, sl, send.at[k], recv.at[k], at_y(k))

    for k in FAR_FIRST:
        scatter(cs, cr, a_s, a_r, k).start()
    for k in FAR_FIRST:
        scattered(cs, cr, a_s, a_r, k).wait_recv()
    total = cs[y].astype(F32)
    for k in range(1, 8):
        total += cr[wrap(y - k, YN)].astype(F32)
    lanes = lax.broadcasted_iota(jnp.int32, (32, 128), 1)
    masks = []
    for c in range(CAP):
        spot = lanes - 64 - 8 * c
        masks.append((lanes < 64) | ((spot >= 0) & (spot < meta[8 + c])))
    cross = jnp.concatenate(
        [jnp.where(masks[c], jnp.exp(total[32 * c : 32 * c + 32] * (HEAD_DIM**-0.5)), 0.0) for c in range(CAP)], axis=0
    )
    den = jnp.sum(cross, axis=1, keepdims=True)
    cwg[y] = cross.astype(BF16)
    sl = cwg.at[y]
    for k in FAR_FIRST:
        remote(sl, sl, b_s.at[k], b_r.at[k], at_y(k)).start()
    load_v.wait()
    for k in FAR_FIRST:
        scattered(cwg, cwg, b_s, b_r, k).wait_recv()

    mixed = []
    for c in range(CAP):
        cw = jnp.concatenate([cwg[g, 32 * c : 32 * c + 32] for g in range(YN)], axis=0)
        mixed.append(jnp.dot(cw, ekeys[c], preferred_element_type=F32).astype(BF16))
    for g in range(YN):
        left = jnp.concatenate([mixed[c][32 * g : 32 * g + 32] for c in range(CAP)], axis=0)
        product = jnp.dot(left, dwv[:, 256 * g : 256 * g + 256], preferred_element_type=F32)
        rows = []
        for c in range(CAP):
            row = jnp.zeros((8, 256), F32)
            for h in range(4):
                low = 32 * c + 8 * h
                row += jnp.where(lane_head == h, product[low : low + 8], 0.0)
            rows.append(row)
        rows.append(jnp.zeros((8, 256), F32))
        ns[g] = jnp.concatenate(rows, axis=0).astype(BF16)
    for k in FAR_FIRST:
        scatter(ns, nr, n_s, n_r, k).start()
    for k in FAR_FIRST:
        scattered(ns, nr, n_s, n_r, k).wait_recv()
    num = ns[y].astype(F32)
    for k in range(1, 8):
        num += nr[wrap(y - k, YN)].astype(F32)

    packed = []
    for c in range(CAP):
        wide = jnp.zeros((8, 256), F32)
        for h in range(4):
            low = 32 * c + 8 * h
            wide = jnp.where(lane_head == h, den[low : low + 8], wide)
        packed.append(jnp.concatenate([num[8 * c : 8 * c + 8], wide], axis=0))
    for spot in range(8):
        for zz in range(ZN):
            question = zz * 8 + spot
            value = jnp.zeros((16, 256), F32)
            for c in range(CAP):
                value += jnp.where(meta[12 + c] == question, packed[c], 0.0)
            t1s[spot, zz] = value.astype(BF16)
    for k in FAR_FIRST:
        remote(t1s.at[lax.rem(r8 + k, 8)], t1r.at[r8], f_s.at[k], f_r.at[k], at_xc(k)).start()
    for k in FAR_FIRST:
        sl = t1r.at[lax.rem(r8 + 8 - k, 8)]
        remote(sl, sl, f_s.at[k], f_r.at[k], at_xc(k)).wait_recv()
    gathered = t1s[r8].astype(F32)
    for k in range(1, 8):
        gathered += t1r[lax.rem(r8 + 8 - k, 8)].astype(F32)
    t2s[...] = gathered.astype(BF16)
    for k in FAR_FIRST:
        remote(t2s.at[wrap(z + k, ZN)], t2r.at[z], h_s.at[k], h_r.at[k], at_z(k)).start()
    for k in FAR_FIRST:
        sl = t2r.at[wrap(z - k, ZN)]
        remote(sl, sl, h_s.at[k], h_r.at[k], at_z(k)).wait_recv()
    answer = t2s[z].astype(F32)
    for k in range(1, 8):
        answer += t2r[wrap(z - k, ZN)].astype(F32)
    out[0] = (answer[0:8] / answer[8:16]).astype(BF16)

    for role in (0, 1):

        @pl.when(core == role)
        def _():
            for number, half in enumerate(sends[role]):
                sl = wg.at[0] if half is None else wg.at[0, pl.ds(0, 32)]
                remote(sl, sl, ring_send.at[number], sib_recv.at[0], sibling).wait_send()

    @pl.when(has_swap)
    def _():
        w_swap().wait_send()

    q_s(core).wait_send()
    w_s(core).wait_send()
    for k in (1, 2, 3):
        q_x(k, x).wait_send()
        w_x(k, x).wait_send()
    for c in range(CAP):
        for sign in (1, -1):
            for step in range(1, YN // 2 + 1):
                y_copy(c, sign, step, y).wait_send()
    for part in range(2):
        for slot in (1, 2, 4, 5, 6, 7, 8, 9):
            sl = ctx_copy(part, 0, y, None if slot < 8 else 0)
            remote(sl, sl, cx_s.at[part, slot], cx_r.at[part, slot], at_y(1)).wait_send()
    for k in range(1, 8):
        q_z(k, z).wait_send()
        w_z(k, z).wait_send()
        for copy in q_y(k, y):
            copy.wait_send()
        scatter(cs, cr, a_s, a_r, k).wait_send()
        scatter(cwg, cwg, b_s, b_r, k).wait_send()
        scatter(ns, nr, n_s, n_r, k).wait_send()
        remote(t1s.at[0], t1r.at[0], f_s.at[k], f_r.at[k], at_xc(k)).wait_send()
        remote(t2s.at[0], t2r.at[0], h_s.at[k], h_r.at[k], at_z(k)).wait_send()


def routing(passage_ids, location, question_lengths, mem_index):
    request_total = passage_ids.size
    pass_count = passage_ids.shape[1]
    row = jnp.take(location, passage_ids.reshape(-1))
    served = row // 4 == mem_index
    order = jnp.arange(request_total)
    rank = jnp.sum((served[None, :] & (order[None, :] < order[:, None])).astype(jnp.int32), axis=1)
    taken = served[None, :] & (rank[None, :] == jnp.arange(4)[:, None])
    question = order // pass_count
    lengths = jnp.broadcast_to(question_lengths[:, None], passage_ids.shape).reshape(-1)
    spot = ((question % 2) * XN + (question // 2) % XN) * ZN + question // (2 * XN)

    def pick(values, empty):
        return jnp.sum(jnp.where(taken, values[None, :] - empty, 0), axis=1) + empty

    return jnp.concatenate(
        [pick(row % 4, 0), pick(spot, 0), pick(lengths, 0), pick(question, -1)]
    ).astype(jnp.int32)


def body(
    question_states, passage_cache, norm_gain, enc_wq, enc_wk, enc_wv, enc_wo, dec_wk, dec_wv, dec_queries,
    passage_ids, location, question_lengths,
):
    meta = routing(passage_ids, location, question_lengths, lax.axis_index("mem"))
    vmem = pl.BlockSpec(memory_space=pltpu.VMEM)
    anywhere = pl.BlockSpec(memory_space=pl.ANY)
    dma = pltpu.SemaphoreType.DMA
    return pl.pallas_call(
        kernel,
        name="step",
        out_shape=jax.ShapeDtypeStruct((1, 8, 256), BF16),
        in_specs=[pl.BlockSpec(memory_space=pltpu.SMEM)] + [vmem] * 7 + [anywhere] * 2 + [vmem],
        out_specs=vmem,
        scratch_shapes=[
            pltpu.VMEM((64, 64, 768), BF16),
            pltpu.VMEM((64, 64, 256), BF16),
            pltpu.VMEM((64, 256), BF16),
            pltpu.VMEM((8, 224, 512), BF16),
            pltpu.VMEM((64, 16, 384), BF16),
            pltpu.VMEM((8, 32, 256), BF16),
            pltpu.VMEM((224, 4096), BF16),
            pltpu.VMEM((8, 2, 224, 128), BF16),
            pltpu.VMEM((224, 512), BF16),
            pltpu.VMEM((3, 128, 512), BF16),
            pltpu.VMEM((3, 256, 512), BF16),
            pltpu.VMEM((8, 96, 128), BF16),
            pltpu.VMEM((8, 96, 128), BF16),
            pltpu.VMEM((8, 96, 128), BF16),
            pltpu.VMEM((8, 32, 256), BF16),
            pltpu.VMEM((8, 32, 256), BF16),
            pltpu.VMEM((8, 8, 16, 256), BF16),
            pltpu.VMEM((8, 8, 16, 256), BF16),
            pltpu.VMEM((8, 16, 256), BF16),
            pltpu.VMEM((8, 16, 256), BF16),
            pltpu.VMEM((512, 2048), BF16),
            pltpu.VMEM((512, 2048), BF16),
            dma((2,)),
            dma((80,)),
            dma((2, 5)),
            dma((8, 2, 5)),
            dma((32,)),
            dma((3, 2, 5)),
            dma((3, 2, 5)),
            dma((8,)), dma((8,)), dma((4,)), dma((4,)), dma((1,)), dma((1,)), dma((2, 8)), dma((2, 8)),
            dma((1,)), dma((1,)), dma((8,)), dma((8,)), dma((4,)), dma((4,)), dma((1,)), dma((1,)),
            dma((2, 10)), dma((2, 10)),
            dma((8,)), dma((8,)), dma((8,)), dma((8,)), dma((8,)), dma((8,)), dma((8,)), dma((8,)), dma((8,)), dma((8,)),
        ],
        compiler_params=pltpu.CompilerParams(
            collective_id=0, has_side_effects=True, vmem_limit_bytes=56 * 2**20
        ),
    )(
        meta, question_states, passage_cache, norm_gain.reshape(8, 512), enc_wq, enc_wk, enc_wv, enc_wo,
        dec_wk, dec_wv, dec_queries,
    )


def solution(mesh):
    in_specs = (
        P("mem", None, "dec"),
        P("mem", None, "dec"),
        P(),
        P("mem", "dec"),
        P("mem", "dec"),
        P("mem", "dec"),
        P("dec", "mem"),
        P("dec", None),
        P("dec", None),
        P("mem", None, "dec"),
        P(),
        P(),
        P(),
    )
    return jax.shard_map(body, mesh=mesh, in_specs=in_specs, out_specs=P("mem", None, "dec"), check_vma=False)
```

time: 617 us -> 110 us (0.18)
  waiting for transfers between devices: 434 us -> 0 us
  blocking collectives: 108 us -> 0 us
  Pallas kernels: 0 us -> 101 us
  starting transfers between devices: 22.5 us -> 0 us
  matrix products: 18.6 us -> 0 us
  between operations: 13.8 us -> 0.07 us
    all_gather x5 -> x0, waiting for transfers between devices: 360 us -> none  [the longest x1 85.7 us: body(): lax.all_gather(enc_wq, 'mem', axis=0, tiled=True)]
    all_gather x2 -> x0, blocking collectives: 108 us -> none  [the longest x1 57.7 us: body(): lax.all_gather(question_states, 'mem', axis=0, tiled=True)]
    pallas_call x0 -> x1, Pallas kernels: none -> 101 us  [body(): pl.pallas_call(kernel, name='step', out_shape=jax.ShapeDtypeStruct((1, 8,...]
    reduce_scatter x3 -> x0, waiting for transfers between devices: 54.6 us -> none  [the longest x1 36.2 us: body(): lax.psum_scatter(partial_out.astype(jnp.bfloat16), 'dec', scatter_dimensi...]
    all_to_all x2 -> x0, starting transfers between devices: 22.3 us -> none  [the longest x1 15.1 us: body(): lax.all_to_all(back_numer.astype(jnp.bfloat16), 'mem', split_axis=0, conc...]
    dot_general x12 -> x0, matrix products: 18.6 us -> none  [the longest x3 8.31 us: body(): jnp.dot(flattened, weight_piece, preferred_element_type=jnp.float32)]
    all_to_all x2 -> x0, waiting for transfers between devices: 17.4 us -> none  [the longest x1 17.4 us: body(): lax.all_to_all(back_numer.astype(jnp.bfloat16), 'mem', split_axis=0, conc...]
  transfers between devices with their start and end apart: 10 -> 0, of which waited for: 8 -> 0; matrix products, arithmetic and copies ran while one was open for 4% -> 0% of each run, Pallas kernels for 0% -> 0%
where the time goes in v1:
time: 110 us; the launch traced here: 109 us
  Pallas kernels  101 us (92%)
  local copies, waits for them, and re-layouts  7.27 us (7%)
    pallas_call x1, Pallas kernels, body(): pl.pallas_call(kernel, name='step', out_shape=jax.ShapeDtypeStruct((1, 8,...  101 us
    unnamed x5, local copies, waits for them, and re-layouts  3.52 us

profile of v1, /device:TPU:1, one launch (start us, length us, event | category | flops | bytes accessed | tf_op | source)
XLA Modules:
  0.0 109.2 jit_solution(10466526763078419869)
XLA Ops:
  0.0 0.0 copy-start
  0.0 1.3 %reshape.170.gain = f32[8,512]{1,0:T(8,128)} reshape(f32[4096]{0:T(1024)} %param.15) | data formatting | bytes 32768 | tf_op jit(solution)/shard_map/reshape | solution.py:628
  1.3 0.8 copy.20
  2.1 0.1 reshape.169
  2.2 0.1 reshape.168
  2.4 0.0 copy-done
  2.4 1.3 %gather_fusion = s32[128]{0:T(128)S(1)} fusion(s32[256]{0:T(256)S(1)} %copy-done, s32[1024]{0:T(1024)S(1)} %pad_clamp_fusion), kind=kCustom, calls=%fused_computation | custom fusion | bytes 1536 | tf_op jit(solution)/shard_map/jit(_take)/gather | solution.py:558
  3.7 0.1 convert_reduce_fusion
  3.8 0.7 broadcast_in_dim.57
  4.6 0.1 broadcast_in_dim.58
  4.7 0.2 select_reduce_fusion.3
  4.9 0.6 pad_add_fusion.meta
  5.5 1.5 %copy.22.wo = bf16[256,64]{1,0:T(8,128)(2,1)} copy(bf16[256,64]{0,1:T(8,128)(2,1)} %param.19) | data formatting | bytes 65536 | tf_op args[6]
  7.0 101.0 %step.1 = bf16[1,8,256]{2,1,0:T(8,128)(2,1)} custom-call(s32[16]{0:T(128)} %pad_add_fusion.meta, bf16[1,8,512]{2,1,0:T(8,128)(2,1)} %qs.1, bf16[4,64,512]{2,1,0:T(8,128)(2,1)} %cache.1, f32[8,512]{1,0:T(8,128)} %reshape.170.gain, bf16[64,256]{1,0:T(8,128)(2,1)} %wq.1, bf16[64,256]{1,0:T(8,128)(2,1)} %wk.1, bf16[64,256]{1,0:T(8,128)(2,1)} %wv.1, ...), custom_call_target="tpu_custom_call" | custom-call | tf_op jit(solution)/shard_map/step/pallas_call | solution.py:583
  108.0 1.3 %copy.24 = bf16[1,8,256]{2,1,0:T(8,128)(2,1)} copy(bf16[1,8,256]{2,1,0:T(8,128)(2,1)} %step.1) | data formatting | bytes 8192
  (6 shorter events, 0.1 us)
Async XLA Ops:
  0.0 2.4 %copy-start = (s32[256]{0:T(256)S(1)}, s32[256]{0:T(256)}, u32[]{:S(2)}) copy-start(s32[256]{0:T(256)} %param.24) | copy-start | bytes 3076

commit v2 on v1

--- a/solution.py
+++ b/solution.py
@@ -11,6 +11,8 @@
 BF16, F32 = jnp.bfloat16, jnp.float32
 ZN, XN, YN = 8, 4, 8
 CAP = 3
+SUBS = 1
+DIRECT = ((False, False), (False, False))
 HEAD_DIM = 64
 NORM_EPSILON = 1e-06
 FAR_FIRST = (4, 3, 5, 2, 6, 1, 7)
@@ -26,7 +28,7 @@
 
 
 def kernel(
-    meta, qs, cache, gain, wq, wk, wv, wo, dwk_hbm, dwv_hbm, dq,
+    ids, rows_of, lengths, qs, cache, gain, wq, wk, wv, wo, dwk_hbm, dwv_hbm, dq,
     out,
     wg, wot, wot_own, xg, qg, dqg, xn, ctxg, enc, ekeys, dqp, cs, cr, cwg, ns, nr, t1s, t1r, t2s, t2r, dwk, dwv,
     load_sem, ring_send, ring1, ring2, sib_recv, yx_send, yx_recv,
@@ -86,16 +88,31 @@
     own_q = (core * XN + x) * ZN + z
     qg[own_q] = jnp.concatenate([first[:, 0:384], second], axis=0).astype(BF16)
     wg[m] = jnp.concatenate([wq[...], wk[...], wv[...]], axis=1)
-    turned = jnp.transpose(wo[...].astype(F32)).astype(BF16)
-    wot_own[...] = turned
+    wot_own[...] = wo[...]
     own_w = (core * XN + x) * ZN + z
 
     @pl.when(jnp.logical_not(has_swap))
     def _():
         wot[own_w] = wot_own[...]
 
+    def look(index, found):
+        count, slots, asking = found
+        question, pick = index // 2, lax.rem(index, 2)
+        place = rows_of[ids[pick, question]] - 4 * m
+        hit = (place >= 0) & (place < 4)
+        taken = [hit & (count == c) for c in range(CAP)]
+        return (
+            count + jnp.where(hit, 1, 0),
+            tuple(jnp.where(taken[c], place, slots[c]) for c in range(CAP)),
+            tuple(jnp.where(taken[c], question, asking[c]) for c in range(CAP)),
+        )
+
+    zero, none = jnp.int32(0), jnp.int32(-1)
+    _, slots, asking = lax.fori_loop(0, 2 * 64, look, (zero, (zero,) * CAP, (none,) * CAP), unroll=8)
+    asked_question = [jnp.maximum(asking[c], 0) for c in range(CAP)]
+    length_of = [lengths[asked_question[c]] for c in range(CAP)]
     for c in range(CAP):
-        xg[y, 64 * c : 64 * c + 64, :] = cache[meta[c]]
+        xg[y, 64 * c : 64 * c + 64, :] = cache[slots[c]]
 
     @pl.when(has_swap)
     def _():
@@ -117,13 +134,9 @@
         sl = qg.at[pl.ds(cc * (XN * ZN), XN * ZN)]
         return remote(sl, sl, qs_s.at[0], qs_r.at[0], sibling)
 
-    def q_y(k, source):
-        sl = xg.at[wrap(source, YN), pl.ds(192, 32)]
-        sd = dqg.at[wrap(source, YN)]
-        return (
-            remote(sl, sl, qy_s.at[0, k], qy_r.at[0, k], at_y(k)),
-            remote(sd, sd, qy_s.at[1, k], qy_r.at[1, k], at_y(k)),
-        )
+    def q_y(which, k, source):
+        sl = (dqg.at[wrap(source, YN)], xg.at[wrap(source, YN), pl.ds(192, 32)])[which]
+        return remote(sl, sl, qy_s.at[which, k], qy_r.at[which, k], at_y(k))
 
     def question_0():
         for k in FAR_FIRST:
@@ -144,21 +157,21 @@
         q_s(1 - core).wait_recv()
         rows, queries = [], []
         for c in range(CAP):
-            asked = qg[meta[4 + c]].astype(F32)
+            q = asked_question[c]
+            asked = qg[(lax.rem(q, 2) * XN + lax.rem(q // 2, XN)) * ZN + q // (2 * XN)].astype(F32)
             rows.append(jnp.concatenate([asked[0:8], asked[8:16, 0:128]], axis=1))
             queries.append(asked[8:16, 128:384])
         rows.append(jnp.zeros((8, 512), F32))
         queries.append(jnp.zeros((8, 256), F32))
         xg[y, 192:224, :] = jnp.concatenate(rows, axis=0).astype(BF16)
         dqg[y] = jnp.concatenate(queries, axis=0).astype(BF16)
+        for which in (1, 0):
+            for k in FAR_FIRST:
+                q_y(which, k, y).start()
+
+    def question_end(which):
         for k in FAR_FIRST:
-            for copy in q_y(k, y):
-                copy.start()
-
-    def question_end():
-        for k in FAR_FIRST:
-            for copy in q_y(k, y - k):
-                copy.wait_recv()
+            q_y(which, k, y - k).wait_recv()
 
     def w_swap():
         return remote(wot_own, wot.at[(lax.rem(r8, 2) * XN + r8 // 2) * ZN + y], wp_s.at[0], wp_r.at[0], swap)
@@ -218,85 +231,89 @@
     def weights(role):
         n1, n2 = (ZN, XN) if role == 0 else (XN, ZN)
         i1, i2 = (z, x) if role == 0 else (x, z)
+        direct_1, direct_2 = DIRECT[role]
         sends = []
 
-        def near(dim, sign):
+        def away(dim, distance):
             along_z = (dim == 1) == (role == 0)
-            return at_z(sign) if along_z else at_x(sign)
+            return at_z(distance) if along_z else at_x(distance)
 
         def chip(o, p):
             a, b = wrap(i1 + o, n1), wrap(i2 + p, n2)
             return a * XN + b if role == 0 else b * XN + a
 
-        def view(o, p, half):
-            index = chip(o, p) * 2 + role
-            return wg.at[index] if half is None else wg.at[index, pl.ds(32 * half, 32)]
-
-        def copy(o, p, half, recv, to, number):
-            sl = view(o, p, half)
+        def copy(o, p, sub, half, recv, to, number):
+            rows = 64 // SUBS
+            low = sub * rows
+            if half is not None:
+                rows = rows // 2
+                low += half * rows
+            sl = wg.at[chip(o, p) * 2 + role, pl.ds(low, rows)]
             return remote(sl, sl, ring_send.at[number], recv, to)
 
-        def start(o, p, half, recv, to):
-            copy(o, p, half, recv, to, len(sends)).start()
+        def start(o, p, sub, half, recv, to):
+            copy(o, p, sub, half, recv, to, len(sends)).start()
             sends.append(half)
 
-        def hand_over(o, p):
-            start(o, p, None, sib_recv.at[chip(o, p)], sibling)
-
-        def half_of(sign):
+        def hand_over(o, p, sub):
+            start(o, p, sub, None, sib_recv.at[chip(o, p), sub], sibling)
+
+        def way(sign):
             return 0 if sign > 0 else 1
 
-        def pass_on(dim, o, p, sign, step):
-            count = n1 if dim == 1 else n2
-            half = half_of(sign) if step == count // 2 else None
-            recv = ring1.at[half_of(sign), step] if dim == 1 else ring2.at[o % n1, half_of(sign), step]
-            start(o, p, half, recv, near(dim, sign))
-
-        def arrived(dim, o, p, sign, step):
-            count = n1 if dim == 1 else n2
-            half = half_of(sign) if step == count // 2 else None
-            recv = ring1.at[half_of(sign), step] if dim == 1 else ring2.at[o % n1, half_of(sign), step]
-            copy(o, p, half, recv, near(dim, sign), 0).wait_recv()
-
-        def second(o):
-            for sign in (1, -1):
-                pass_on(2, o, 0, sign, 1)
-            hand_over(o, 0)
-
-        def arrive_1(step):
-            for sign in (1, -1):
-                arrived(1, -sign * step, 0, sign, step)
-                if step < n1 // 2:
-                    pass_on(1, -sign * step, 0, sign, step + 1)
-                    second(-sign * step)
-            if step == n1 // 2:
-                second(step)
-
-        def arrive_2(o, step):
-            for sign in (1, -1):
-                arrived(2, o, -sign * step, sign, step)
-                if step < n2 // 2:
-                    pass_on(2, o, -sign * step, sign, step + 1)
-                    hand_over(o, -sign * step)
-            if step == n2 // 2:
-                hand_over(o, step)
+        def receipt(dim, o, sign, step, sub):
+            return ring1.at[way(sign), step, sub] if dim == 1 else ring2.at[o % n1, way(sign), step, sub]
+
+        def half_at(dim, sign, step):
+            count, direct = (n1, direct_1) if dim == 1 else (n2, direct_2)
+            return way(sign) if step == count // 2 and not direct else None
+
+        def spread(dim, o, sub):
+            count, direct = (n1, direct_1) if dim == 1 else (n2, direct_2)
+            if not direct:
+                for sign in (1, -1):
+                    start(o, 0, sub, half_at(dim, sign, 1), receipt(dim, o, sign, 1, sub), away(dim, sign))
+                return
+            for step in range(count // 2, 0, -1):
+                for sign in (1, -1) if step < count // 2 else (1,):
+                    start(o, 0, sub, None, receipt(dim, o, sign, step, sub), away(dim, sign * step))
+
+        def arrive(dim, o, sign, step, sub):
+            count, direct = (n1, direct_1) if dim == 1 else (n2, direct_2)
+            last = step == count // 2
+            if direct and last and sign < 0:
+                return False
+            place = (-sign * step, 0) if dim == 1 else (o, -sign * step)
+            half = half_at(dim, sign, step)
+            copy(*place, sub, half, receipt(dim, o, sign, step, sub), away(dim, sign), 0).wait_recv()
+            if not direct and not last:
+                onward = half_at(dim, sign, step + 1)
+                start(*place, sub, onward, receipt(dim, o, sign, step + 1, sub), away(dim, sign))
+            return not last or direct or sign < 0
 
         for time in range(n1 // 2 + n2 // 2 + 1):
             if time == 0:
                 question_0()
                 wout_0()
-                for sign in (1, -1):
-                    pass_on(1, 0, 0, sign, 1)
-                second(0)
-            elif time <= n1 // 2:
-                arrive_1(time)
-            if time <= YN // 2:
-                rows_step(time)
-            for step in range(1, n2 // 2 + 1):
-                o = time - step
-                if 0 <= o <= n1 // 2:
-                    for signed in (o,) if o in (0, n1 // 2) else (o, -o):
-                        arrive_2(signed, step)
+            for sub in range(SUBS):
+                if time == 0:
+                    spread(1, 0, sub)
+                    spread(2, 0, sub)
+                    hand_over(0, 0, sub)
+                elif time <= n1 // 2:
+                    for sign in (1, -1):
+                        if arrive(1, 0, sign, time, sub):
+                            spread(2, -sign * time, sub)
+                            hand_over(-sign * time, 0, sub)
+                if time <= YN // 2 and sub == 0:
+                    rows_step(time)
+                for step in range(1, n2 // 2 + 1):
+                    o = time - step
+                    if 0 <= o <= n1 // 2:
+                        for signed in (o,) if o in (0, n1 // 2) else (o, -o):
+                            for sign in (1, -1):
+                                if arrive(2, signed, sign, step, sub):
+                                    hand_over(signed, -sign * step, sub)
             if time == 1:
                 question_1()
             if time == 2:
@@ -315,24 +332,31 @@
             sends[role] = weights(role)
 
     for chip in range(ZN * XN):
-        sl = wg.at[chip * 2 + (1 - core)]
-        remote(sl, sl, ring_send.at[0], sib_recv.at[chip], sibling).wait_recv()
-    question_end()
+        for sub in range(SUBS):
+            sl = wg.at[chip * 2 + (1 - core), pl.ds(64 // SUBS * sub, 64 // SUBS)]
+            remote(sl, sl, ring_send.at[0], sib_recv.at[chip, sub], sibling).wait_recv()
     wout_2()
 
-    squares = jnp.zeros((224, 128), F32)
-    for d in range(YN):
-        block = xg[d].astype(F32)
-        block = block * block
-        squares += block[:, 0:128] + block[:, 128:256] + block[:, 256:384] + block[:, 384:512]
-    inverse = lax.rsqrt(jnp.sum(squares, axis=1, keepdims=True) * (1.0 / (512 * YN)) + NORM_EPSILON)
-    for d in range(YN):
-        xn[:, 512 * d : 512 * d + 512] = (xg[d].astype(F32) * inverse * gain[d : d + 1, :]).astype(BF16)
-    totals = []
-    for part in range(3):
-        weight = wg[:, :, 256 * part : 256 * part + 256].reshape(4096, 256)
-        totals.append(jnp.dot(xn[...], weight, preferred_element_type=F32).astype(BF16))
-    queries, keys, values = totals
+    def project(low, high):
+        squares = jnp.zeros((high - low, 128), F32)
+        for d in range(YN):
+            block = xg[d, low:high, :].astype(F32)
+            block = block * block
+            squares += block[:, 0:128] + block[:, 128:256] + block[:, 256:384] + block[:, 384:512]
+        inverse = lax.rsqrt(jnp.sum(squares, axis=1, keepdims=True) * (1.0 / (512 * YN)) + NORM_EPSILON)
+        for d in range(YN):
+            scale = jnp.concatenate([gain[4 * d + part : 4 * d + part + 1, :] for part in range(4)], axis=1)
+            xn[low:high, 512 * d : 512 * d + 512] = (xg[d, low:high, :].astype(F32) * inverse * scale).astype(BF16)
+        totals = []
+        for part in range(3):
+            weight = wg[:, :, 256 * part : 256 * part + 256].reshape(4096, 256)
+            totals.append(jnp.dot(xn[low:high, :], weight, preferred_element_type=F32).astype(BF16))
+        return totals
+
+    first_rows = project(0, 192)
+    question_end(1)
+    last_rows = project(192, 224)
+    queries, keys, values = (jnp.concatenate(both, axis=0) for both in zip(first_rows, last_rows))
 
     def pair_of(index):
         return jnp.where(index < 192, index // 64, jnp.minimum((index - 192) // 8, CAP - 1))
@@ -340,7 +364,7 @@
     row_ids = lax.broadcasted_iota(jnp.int32, (224, 224), 0)
     col_ids = lax.broadcasted_iota(jnp.int32, (224, 224), 1)
     col_pair = pair_of(col_ids)
-    length = jnp.where(col_pair == 0, meta[8], jnp.where(col_pair == 1, meta[9], meta[10]))
+    length = jnp.where(col_pair == 0, length_of[0], jnp.where(col_pair == 1, length_of[1], length_of[2]))
     token = col_ids - 192 - 8 * col_pair
     live = (pair_of(row_ids) == col_pair) & (token < length)
 
@@ -386,6 +410,7 @@
         remote(sl, sl, cx_s.at[part, slot], cx_r.at[part, slot], at_y(2 * sign)).start()
 
     load_k.wait()
+    question_end(0)
     lane_head = lax.broadcasted_iota(jnp.int32, (8, 256), 1) // 64
     for g in range(YN):
         asked = dqg[g].astype(F32)
@@ -445,7 +470,7 @@
     masks = []
     for c in range(CAP):
         spot = lanes - 64 - 8 * c
-        masks.append((lanes < 64) | ((spot >= 0) & (spot < meta[8 + c])))
+        masks.append((lanes < 64) | ((spot >= 0) & (spot < length_of[c])))
     cross = jnp.concatenate(
         [jnp.where(masks[c], jnp.exp(total[32 * c : 32 * c + 32] * (HEAD_DIM**-0.5)), 0.0) for c in range(CAP)], axis=0
     )
@@ -494,7 +519,7 @@
             question = zz * 8 + spot
             value = jnp.zeros((16, 256), F32)
             for c in range(CAP):
-                value += jnp.where(meta[12 + c] == question, packed[c], 0.0)
+                value += jnp.where(asking[c] == question, packed[c], 0.0)
             t1s[spot, zz] = value.astype(BF16)
     for k in FAR_FIRST:
         remote(t1s.at[lax.rem(r8 + k, 8)], t1r.at[r8], f_s.at[k], f_r.at[k], at_xc(k)).start()
@@ -520,8 +545,8 @@
         @pl.when(core == role)
         def _():
             for number, half in enumerate(sends[role]):
-                sl = wg.at[0] if half is None else wg.at[0, pl.ds(0, 32)]
-                remote(sl, sl, ring_send.at[number], sib_recv.at[0], sibling).wait_send()
+                sl = wg.at[0, pl.ds(0, 64 // SUBS if half is None else 32 // SUBS)]
+                remote(sl, sl, ring_send.at[number], sib_recv.at[0, 0], sibling).wait_send()
 
     @pl.when(has_swap)
     def _():
@@ -543,8 +568,8 @@
     for k in range(1, 8):
         q_z(k, z).wait_send()
         w_z(k, z).wait_send()
-        for copy in q_y(k, y):
-            copy.wait_send()
+        for which in (1, 0):
+            q_y(which, k, y).wait_send()
         scatter(cs, cr, a_s, a_r, k).wait_send()
         scatter(cwg, cwg, b_s, b_r, k).wait_send()
         scatter(ns, nr, n_s, n_r, k).wait_send()
@@ -552,31 +577,10 @@
         remote(t2s.at[0], t2r.at[0], h_s.at[k], h_r.at[k], at_z(k)).wait_send()
 
 
-def routing(passage_ids, location, question_lengths, mem_index):
-    request_total = passage_ids.size
-    pass_count = passage_ids.shape[1]
-    row = jnp.take(location, passage_ids.reshape(-1))
-    served = row // 4 == mem_index
-    order = jnp.arange(request_total)
-    rank = jnp.sum((served[None, :] & (order[None, :] < order[:, None])).astype(jnp.int32), axis=1)
-    taken = served[None, :] & (rank[None, :] == jnp.arange(4)[:, None])
-    question = order // pass_count
-    lengths = jnp.broadcast_to(question_lengths[:, None], passage_ids.shape).reshape(-1)
-    spot = ((question % 2) * XN + (question // 2) % XN) * ZN + question // (2 * XN)
-
-    def pick(values, empty):
-        return jnp.sum(jnp.where(taken, values[None, :] - empty, 0), axis=1) + empty
-
-    return jnp.concatenate(
-        [pick(row % 4, 0), pick(spot, 0), pick(lengths, 0), pick(question, -1)]
-    ).astype(jnp.int32)
-
-
 def body(
     question_states, passage_cache, norm_gain, enc_wq, enc_wk, enc_wv, enc_wo, dec_wk, dec_wv, dec_queries,
     passage_ids, location, question_lengths,
 ):
-    meta = routing(passage_ids, location, question_lengths, lax.axis_index("mem"))
     vmem = pl.BlockSpec(memory_space=pltpu.VMEM)
     anywhere = pl.BlockSpec(memory_space=pl.ANY)
     dma = pltpu.SemaphoreType.DMA
@@ -584,7 +588,7 @@
         kernel,
         name="step",
         out_shape=jax.ShapeDtypeStruct((1, 8, 256), BF16),
-        in_specs=[pl.BlockSpec(memory_space=pltpu.SMEM)] + [vmem] * 7 + [anywhere] * 2 + [vmem],
+        in_specs=[pl.BlockSpec(memory_space=pltpu.SMEM)] * 3 + [vmem] * 7 + [anywhere] * 2 + [vmem],
         out_specs=vmem,
         scratch_shapes=[
             pltpu.VMEM((64, 64, 768), BF16),
@@ -610,10 +614,10 @@
             pltpu.VMEM((512, 2048), BF16),
             pltpu.VMEM((512, 2048), BF16),
             dma((2,)),
-            dma((80,)),
-            dma((2, 5)),
-            dma((8, 2, 5)),
-            dma((32,)),
+            dma((80 * SUBS,)),
+            dma((2, 5, SUBS)),
+            dma((8, 2, 5, SUBS)),
+            dma((32, SUBS)),
             dma((3, 2, 5)),
             dma((3, 2, 5)),
             dma((8,)), dma((8,)), dma((4,)), dma((4,)), dma((1,)), dma((1,)), dma((2, 8)), dma((2, 8)),
@@ -625,7 +629,8 @@
             collective_id=0, has_side_effects=True, vmem_limit_bytes=56 * 2**20
         ),
     )(
-        meta, question_states, passage_cache, norm_gain.reshape(8, 512), enc_wq, enc_wk, enc_wv, enc_wo,
+        passage_ids.T, location, question_lengths, question_states, passage_cache, norm_gain.reshape(32, 128),
+        enc_wq, enc_wk, enc_wv, enc_wo.T,
         dec_wk, dec_wv, dec_queries,
     )
 

time: 110 us -> 103 us (0.936)
  local copies, waits for them, and re-layouts: 7.27 us -> 1.28 us
    unnamed x5 -> x1, local copies, waits for them, and re-layouts: 3.52 us -> 1.28 us
    reshape x3 -> x0, local copies, waits for them, and re-layouts: 1.6 us -> none  [the longest x1 1.32 us: body(): norm_gain.reshape(8, 512)]
    gather x1 -> x0, local copies, waits for them, and re-layouts: 1.27 us -> none  [routing(): row = jnp.take(location, passage_ids.reshape(-1))]
where the time goes in v2:
time: 103 us
  Pallas kernels  102 us (99%)
  local copies, waits for them, and re-layouts  1.28 us (1%)
    pallas_call x1, Pallas kernels, body(): pl.pallas_call(kernel, name='step', out_shape=jax.ShapeDtypeStruct((1, 8,...  102 us

profile of v2, /device:TPU:1, one launch (start us, length us, event | category | flops | bytes accessed | tf_op | source)
XLA Modules:
  0.0 102.8 jit_solution(16526604231075292551)
XLA Ops:
  0.0 101.5 %step.1 = bf16[1,8,256]{2,1,0:T(8,128)(2,1)} custom-call(s32[2,64]{1,0:T(2,128)} %bitcast.5, s32[256]{0:T(256)} %rows_of.1, s32[64]{0:T(128)} %lengths.1, bf16[1,8,512]{2,1,0:T(8,128)(2,1)} %qs.1, bf16[4,64,512]{2,1,0:T(8,128)(2,1)} %cache.1, f32[32,128]{1,0:T(8,128)} %bitcast.4, bf16[64,256]{1,0:T(8,128)(2,1)} %wq.1, bf16[64,256]{1,0:T(8,128)(2,1)} %wk.1, ...), custom_call_target="tpu_custom_call" | custom-call | tf_op jit(solution)/shard_map/step/pallas_call | solution.py:587
  101.5 1.3 %copy.15 = bf16[1,8,256]{2,1,0:T(8,128)(2,1)} copy(bf16[1,8,256]{2,1,0:T(8,128)(2,1)} %step.1) | data formatting | bytes 8192

commit v3 on v2

v3 whole, which is shorter than its diff:
```python
import functools

import jax
import jax.numpy as jnp
from jax import lax
from jax.experimental import pallas as pl
from jax.experimental.pallas import tpu as pltpu
from jax.sharding import PartitionSpec as P

MESH = pl.DeviceIdType.MESH
BF16, F32 = jnp.bfloat16, jnp.float32
ZN, XN, YN = 8, 4, 8
CAP = 3
MODES = (("hybrid", "ring"), ("direct", "ring"))
(G_QZ, G_QX, G_QS, G_QY, G_DY, G_WP, G_WZ, G_WX, G_WS, G_CTX, G_A, G_B, G_N, G_F, G_H, G_RING, G_ROWS) = range(17)
HEAD_DIM = 64
NORM_EPSILON = 1e-06
FAR_FIRST = (4, 3, 5, 2, 6, 1, 7)
NT = (((1,), (1,)), ((), ()))


def wrap(value, size):
    return lax.rem(value + size, size)


def dot_nt(a, b):
    return lax.dot_general(a, b, NT, preferred_element_type=F32)


def kernel(
    ids_in, rows_in, lengths_in, qs_in, cache_in, gain_in, wq_in, wk_in, wv_in, wo_in, dwk_in, dwv_in, dq_in,
    out,
    ids, rows_of, lengths, qs, cache, gain, dq,
    wg, wot, wot_own, xg, qg, dqg, xn, ctxg, enc, ekeys, dqp, cs, cr, cwg, ns, nr, t1r, t2s, t2r, dwk, dwv,
    load_sem, ring1, ring2, sib_recv, rows_recv, ctx_sem, sent, got,
):
    m = lax.axis_index("mem")
    y = lax.axis_index("dec")
    z = m // (2 * XN)
    x = lax.rem(m // 2, XN)
    core = lax.rem(m, 2)
    r8 = lax.rem(m, 8)

    def device(zz, xx, cc, yy):
        return ((zz * XN + xx) * 2 + cc, yy)

    def at_z(k):
        return device(wrap(z + k, ZN), x, core, y)

    def at_x(k):
        return device(z, wrap(x + k, XN), core, y)

    def at_y(k):
        return device(z, x, core, wrap(y + k, YN))

    def at_xc(k):
        other = lax.rem(r8 + k, 8)
        return (z * 8 + other, y)

    sibling = device(z, x, 1 - core, y)
    swap = (8 * y + r8, z)
    has_swap = z != y

    def remote(src, dst, send, recv, to):
        return pltpu.make_async_remote_copy(
            src_ref=src, dst_ref=dst, send_sem=send, recv_sem=recv, device_id=to, device_id_type=MESH
        )

    def all_sent(group, ref):
        remote(ref, ref, sent.at[group], got.at[group], sibling).wait_send()

    def all_got(group, ref):
        remote(ref, ref, sent.at[group], got.at[group], sibling).wait_recv()

    barrier = pltpu.get_barrier_semaphore()
    for k in range(1, 8):
        pl.semaphore_signal(barrier, inc=1, device_id=at_y(k), device_id_type=MESH)
        pl.semaphore_signal(barrier, inc=1, device_id=at_z(k), device_id_type=MESH)
        pl.semaphore_signal(barrier, inc=1, device_id=at_xc(k), device_id_type=MESH)

    @pl.when(has_swap)
    def _():
        pl.semaphore_signal(barrier, inc=1, device_id=swap, device_id_type=MESH)

    loads = [
        pltpu.make_async_copy(source, target, load_sem.at[number])
        for number, (source, target) in enumerate(
            [
                (ids_in, ids), (rows_in, rows_of), (lengths_in, lengths),
                (cache_in, cache), (qs_in, qs), (dq_in, dq), (wo_in, wot_own), (gain_in, gain),
                (wq_in, wg.at[m, :, pl.ds(0, 256)]),
                (wk_in, wg.at[m, :, pl.ds(256, 256)]),
                (wv_in, wg.at[m, :, pl.ds(512, 256)]),
                (dwk_in, dwk), (dwv_in, dwv),
            ]
        )
    ]
    for load in loads:
        load.start()
    load_k, load_v = loads[11:]

    def look(index, found):
        count, slots, asking = found
        question, pick = index // 2, lax.rem(index, 2)
        place = rows_of[ids[pick, question]] - 4 * m
        hit = (place >= 0) & (place < 4)
        taken = [hit & (count == c) for c in range(CAP)]
        return (
            count + jnp.where(hit, 1, 0),
            tuple(jnp.where(taken[c], place, slots[c]) for c in range(CAP)),
            tuple(jnp.where(taken[c], question, asking[c]) for c in range(CAP)),
        )

    for load in loads[:3]:
        load.wait()
    zero, none = jnp.int32(0), jnp.int32(-1)
    _, slots, asking = lax.fori_loop(0, 2 * 64, look, (zero, (zero,) * CAP, (none,) * CAP), unroll=8)
    asked_question = [jnp.maximum(asking[c], 0) for c in range(CAP)]
    length_of = [lengths[asked_question[c]] for c in range(CAP)]
    for load in loads[3:11]:
        load.wait()
    for c in range(CAP):
        xg[y, 64 * c : 64 * c + 64, :] = cache[slots[c]]

    first = qs[0].astype(F32)
    second = jnp.concatenate([first[:, 384:512], dq[0].astype(F32)], axis=1)
    own_q = (core * XN + x) * ZN + z
    qg[own_q] = jnp.concatenate([first[:, 0:384], second], axis=0).astype(BF16)

    @pl.when(jnp.logical_not(has_swap))
    def _():
        wot[own_q] = wot_own[...]

    @pl.when(has_swap)
    def _():
        pl.semaphore_wait(barrier, 22)

    @pl.when(jnp.logical_not(has_swap))
    def _():
        pl.semaphore_wait(barrier, 21)

    def q_z(k, source):
        sl = qg.at[(core * XN + x) * ZN + wrap(source, ZN)]
        return remote(sl, sl, sent.at[G_QZ], got.at[G_QZ], at_z(k))

    def q_x(k, source):
        sl = qg.at[pl.ds((core * XN + wrap(source, XN)) * ZN, ZN)]
        return remote(sl, sl, sent.at[G_QX], got.at[G_QX], at_x(k))

    def q_s(cc):
        sl = qg.at[pl.ds(cc * (XN * ZN), XN * ZN)]
        return remote(sl, sl, sent.at[G_QS], got.at[G_QS], sibling)

    def q_y(which, k, source):
        sl = (dqg.at[wrap(source, YN)], xg.at[wrap(source, YN), pl.ds(192, 32)])[which]
        group = (G_DY, G_QY)[which]
        return remote(sl, sl, sent.at[group], got.at[group], at_y(k))

    def question_0():
        for k in FAR_FIRST:
            q_z(k, z).start()

    def question_1():
        all_got(G_QZ, qg.at[pl.ds(0, 7)])
        for k in (2, 1, 3):
            q_x(k, x).start()

    def question_2():
        all_got(G_QX, qg.at[pl.ds(0, 24)])
        q_s(core).start()

    def question_3():
        q_s(1 - core).wait_recv()
        rows, queries = [], []
        for c in range(CAP):
            q = asked_question[c]
            asked = qg[(lax.rem(q, 2) * XN + lax.rem(q // 2, XN)) * ZN + q // (2 * XN)].astype(F32)
            rows.append(jnp.concatenate([asked[0:8], asked[8:16, 0:128]], axis=1))
            queries.append(asked[8:16, 128:384])
        rows.append(jnp.zeros((8, 512), F32))
        queries.append(jnp.zeros((8, 256), F32))
        xg[y, 192:224, :] = jnp.concatenate(rows, axis=0).astype(BF16)
        dqg[y] = jnp.concatenate(queries, axis=0).astype(BF16)
        for which in (1, 0):
            for k in FAR_FIRST:
                q_y(which, k, y).start()

    def question_end(which):
        if which:
            all_got(G_QY, xg.at[0])
        else:
            all_got(G_DY, dqg.at[pl.ds(0, 7)])

    def w_swap():
        return remote(wot_own, wot.at[(lax.rem(r8, 2) * XN + r8 // 2) * ZN + y], sent.at[G_WP], got.at[G_WP], swap)

    def w_z(k, source):
        sl = wot.at[(core * XN + x) * ZN + wrap(source, ZN)]
        return remote(sl, sl, sent.at[G_WZ], got.at[G_WZ], at_z(k))

    def w_x(k, source):
        sl = wot.at[pl.ds((core * XN + wrap(source, XN)) * ZN, ZN)]
        return remote(sl, sl, sent.at[G_WX], got.at[G_WX], at_x(k))

    def w_s(cc):
        sl = wot.at[pl.ds(cc * (XN * ZN), XN * ZN)]
        return remote(sl, sl, sent.at[G_WS], got.at[G_WS], sibling)

    def wout_0():
        @pl.when(has_swap)
        def _():
            w_swap().start()

    def wout_1():
        @pl.when(has_swap)
        def _():
            w_swap().wait_recv()

        for k in FAR_FIRST:
            w_z(k, z).start()

    def wout_2():
        all_got(G_WZ, wot.at[pl.ds(0, 7)])
        for k in (2, 1, 3):
            w_x(k, x).start()

    def wout_3():
        all_got(G_WX, wot.at[pl.ds(0, 24)])
        w_s(core).start()

    def y_copy(c, sign, step, source):
        if step < YN // 2:
            sl = xg.at[wrap(source, YN), pl.ds(64 * c, 64)]
        else:
            sl = xg.at[wrap(source, YN), pl.ds(64 * c + (0 if sign > 0 else 32), 32)]
        d = 0 if sign > 0 else 1
        return remote(sl, sl, sent.at[G_ROWS], rows_recv.at[c, d, step], at_y(sign))

    def rows_step(step):
        for c in range(CAP):
            for sign in (1, -1):
                if step > 0:
                    y_copy(c, sign, step, y - sign * step).wait_recv()
                if step < YN // 2:
                    y_copy(c, sign, step + 1, y - sign * step).start()

    def weights(role):
        n1, n2 = (ZN, XN) if role == 0 else (XN, ZN)
        i1, i2 = (z, x) if role == 0 else (x, z)
        mode_1, mode_2 = MODES[role]

        def away(dim, distance):
            return at_z(distance) if (dim == 1) == (role == 0) else at_x(distance)

        def chip(o, p):
            a, b = wrap(i1 + o, n1), wrap(i2 + p, n2)
            return a * XN + b if role == 0 else b * XN + a

        def copy(o, p, half, recv, to):
            index = chip(o, p) * 2 + role
            sl = wg.at[index] if half is None else wg.at[index, pl.ds(32 * half, 32)]
            return remote(sl, sl, sent.at[G_RING], recv, to)

        def hand_over(o, p):
            copy(o, p, None, sib_recv.at[0], sibling).start()

        def way(sign):
            return 0 if sign > 0 else 1

        def receipt(dim, o, sign, step):
            return ring1.at[way(sign), step] if dim == 1 else ring2.at[o % n1, way(sign), step]

        def travel(dim):
            return (n1, mode_1) if dim == 1 else (n2, mode_2)

        def half_at(dim, sign, step):
            count, mode = travel(dim)
            return way(sign) if step == count // 2 and mode != "direct" else None

        def spread(dim, o):
            count, mode = travel(dim)
            if mode == "ring":
                steps = (1,)
            elif mode == "hybrid":
                steps = (2, 1)
            else:
                steps = range(1, count // 2 + 1)
            for step in steps:
                for sign in (1, -1) if mode != "direct" or step < count // 2 else (1,):
                    half = half_at(dim, sign, step)
                    copy(o, 0, half, receipt(dim, o, sign, step), away(dim, sign * step)).start()

        def arrive(dim, o, sign, step):
            count, mode = travel(dim)
            last = step == count // 2
            if mode == "direct" and last and sign < 0:
                return False
            place = (-sign * step, 0) if dim == 1 else (o, -sign * step)
            copy(*place, half_at(dim, sign, step), receipt(dim, o, sign, step), away(dim, sign)).wait_recv()
            if mode == "ring" and not last:
                onward = half_at(dim, sign, step + 1)
                copy(*place, onward, receipt(dim, o, sign, step + 1), away(dim, sign)).start()
            if mode == "hybrid" and step == 2:
                copy(*place, None, receipt(dim, o, sign, 3), away(dim, sign)).start()
                copy(*place, way(sign), receipt(dim, o, sign, 4), away(dim, 2 * sign)).start()
            return not last or mode == "direct" or sign < 0

        def when(mode, step):
            return {"ring": step, "direct": min(step, 1), "hybrid": (step + 1) // 2}[mode]

        def order(mode, count):
            return (2, 1, 3, 4) if mode == "hybrid" else range(1, count // 2 + 1)

        events = [(when(mode_1, step), 0, 1, step, 0) for step in order(mode_1, n1)]
        for o in range(n1 // 2 + 1):
            events += [(when(mode_1, o) + when(mode_2, step), 1, 2, step, o) for step in order(mode_2, n2)]
        events.sort(key=lambda event: event[:2])

        question_0()
        wout_0()
        spread(1, 0)
        spread(2, 0)
        hand_over(0, 0)
        rows_step(0)
        after = {1: question_1, 2: question_2, 3: question_3, 4: wout_1}
        for time in range(1, max(4, events[-1][0]) + 1):
            now = [event for event in events if event[0] == time]
            for _, _, dim, step, o in now:
                if dim == 1:
                    for sign in (1, -1):
                        if arrive(1, 0, sign, step):
                            spread(2, -sign * step)
                            hand_over(-sign * step, 0)
            if time <= YN // 2:
                rows_step(time)
            for _, _, dim, step, o in now:
                if dim == 2:
                    for signed in (o,) if o in (0, n1 // 2) else (o, -o):
                        for sign in (1, -1):
                            if arrive(2, signed, sign, step):
                                hand_over(signed, -sign * step)
            if time in after:
                after[time]()

    for role in (0, 1):

        @pl.when(core == role)
        def _():
            weights(role)

    question_end(1)
    squares = jnp.zeros((224, 128), F32)
    for d in range(YN):
        block = xg[d].astype(F32)
        block = block * block
        squares += block[:, 0:128] + block[:, 128:256] + block[:, 256:384] + block[:, 384:512]
    inverse = lax.rsqrt(jnp.sum(squares, axis=1, keepdims=True) * (1.0 / (512 * YN)) + NORM_EPSILON)
    for d in range(YN):
        scale = jnp.concatenate([gain[4 * d + part : 4 * d + part + 1, :] for part in range(4)], axis=1)
        xn[:, 512 * d : 512 * d + 512] = (xg[d].astype(F32) * inverse * scale).astype(BF16)

    remote(wg.at[pl.ds(0, 32)], wg.at[pl.ds(0, 32)], sent.at[G_RING], sib_recv.at[0], sibling).wait_recv()
    wout_2()
    queries, keys, values = (
        jnp.dot(
            xn[...], wg[:, :, 256 * part : 256 * part + 256].reshape(4096, 256), preferred_element_type=F32
        ).astype(BF16)
        for part in range(3)
    )

    def pair_of(index):
        return jnp.where(index < 192, index // 64, jnp.minimum((index - 192) // 8, CAP - 1))

    row_ids = lax.broadcasted_iota(jnp.int32, (224, 224), 0)
    col_ids = lax.broadcasted_iota(jnp.int32, (224, 224), 1)
    col_pair = pair_of(col_ids)
    length = jnp.where(col_pair == 0, length_of[0], jnp.where(col_pair == 1, length_of[1], length_of[2]))
    token = col_ids - 192 - 8 * col_pair
    live = (pair_of(row_ids) == col_pair) & (token < length)

    def ctx_copy(part, k, source, half):
        if half is None:
            sl = ctxg.at[wrap(source, YN), part]
        else:
            sl = ctxg.at[wrap(source, YN), part, pl.ds(112 * half, 112)]
        return sl

    def ctx_near(part, k):
        sl = ctx_copy(part, k, y, None)
        return remote(sl, sl, sent.at[G_CTX], ctx_sem.at[part, k], at_y(k - 3))

    for part in range(2):
        outs = []
        for h in (2 * part, 2 * part + 1):
            sl = slice(64 * h, 64 * h + 64)
            scores = dot_nt(queries[:, sl], keys[:, sl]) * (HEAD_DIM**-0.5)
            weight = jnp.where(live, jnp.exp(scores), 0.0)
            prob = (weight / jnp.sum(weight, axis=1, keepdims=True)).astype(BF16)
            outs.append(jnp.dot(prob, values[:, sl], preferred_element_type=F32))
        ctxg[y, part] = jnp.concatenate(outs, axis=1).astype(BF16)
        for k in (-2, 2, -1, 1):
            ctx_near(part, k + 3).start()

    def ctx_recv(part, k, half=None):
        sl = ctx_copy(part, k, y - k, half)
        return sl

    def ctx_wait(part, k, half=None):
        sl = ctx_recv(part, k, half)
        slot = k + 3 if abs(k) <= 2 else {3: 6, -3: 7, 4: 8, -4: 9}[k]
        remote(sl, sl, sent.at[G_CTX], ctx_sem.at[part, slot], at_y(1)).wait_recv()

    def ctx_forward(part, sign):
        sl = ctx_copy(part, 0, y - 2 * sign, None)
        slot = 6 if sign > 0 else 7
        remote(sl, sl, sent.at[G_CTX], ctx_sem.at[part, slot], at_y(sign)).start()
        half = 0 if sign > 0 else 1
        sl = ctx_copy(part, 0, y - 2 * sign, half)
        slot = 8 if sign > 0 else 9
        remote(sl, sl, sent.at[G_CTX], ctx_sem.at[part, slot], at_y(2 * sign)).start()

    load_k.wait()
    question_end(0)
    lane_head = lax.broadcasted_iota(jnp.int32, (8, 256), 1) // 64
    for g in range(YN):
        asked = dqg[g].astype(F32)
        blocks = []
        for c in range(CAP):
            for h in range(4):
                blocks.append(jnp.where(lane_head == h, asked[8 * c : 8 * c + 8], 0.0))
        spread = jnp.concatenate(blocks, axis=0).astype(BF16)
        product = dot_nt(spread, dwk[:, 256 * g : 256 * g + 256]).astype(BF16)
        for c in range(CAP):
            dqp[c, 32 * g : 32 * g + 32, :] = product[32 * c : 32 * c + 32]

    all_sent(G_RING, wg.at[pl.ds(0, 63)])
    all_sent(G_ROWS, xg.at[pl.ds(0, 6)])
    all_sent(G_QZ, qg.at[pl.ds(0, 7)])
    all_sent(G_QX, qg.at[pl.ds(0, 24)])
    all_sent(G_QS, qg.at[pl.ds(0, 32)])
    all_sent(G_QY, xg.at[0])
    all_sent(G_DY, dqg.at[pl.ds(0, 7)])
    all_sent(G_WZ, wot.at[pl.ds(0, 7)])

    @pl.when(has_swap)
    def _():
        w_swap().wait_send()

    for part in range(2):
        for sign in (1, -1):
            ctx_wait(part, 2 * sign)
            ctx_forward(part, sign)
    wout_3()
    for part in range(2):
        for sign in (1, -1):
            ctx_wait(part, sign)
            ctx_wait(part, 3 * sign)
            ctx_wait(part, 4 * sign, 0 if sign > 0 else 1)
    w_s(1 - core).wait_recv()

    attended = jnp.zeros((224, 512), F32)
    for d in range(YN):
        context = jnp.concatenate([ctxg[d, 0], ctxg[d, 1]], axis=1)
        weight = jnp.concatenate(
            [wot[((r % 2) * XN + r // 2) * ZN + d] for r in range(8)], axis=0
        )
        attended += dot_nt(context, weight)
    enc[...] = (xg[y].astype(F32) + attended).astype(BF16)

    for c in range(CAP):
        ekeys[c, 0:64, :] = enc[64 * c : 64 * c + 64, :]
        ekeys[c, 64:96, :] = enc[192:224, :]
        ekeys[c, 96:128, :] = jnp.zeros((32, 512), BF16)
        part = dot_nt(dqp[c], ekeys[c]).astype(BF16)
        for g in range(YN):
            cs[g, 32 * c : 32 * c + 32, :] = part[32 * g : 32 * g + 32]

    def scatter(src, dst, group):
        for k in FAR_FIRST:
            remote(src.at[wrap(y + k, YN)], dst.at[y], sent.at[group], got.at[group], at_y(k)).start()

    seven = pl.ds(0, 7)
    scatter(cs, cr, G_A)
    all_sent(G_WX, wot.at[pl.ds(0, 24)])
    all_sent(G_WS, wot.at[pl.ds(0, 32)])
    all_sent(G_CTX, ctxg.at[seven])
    all_got(G_A, cr.at[seven])
    total = cs[y].astype(F32)
    for k in range(1, 8):
        total += cr[wrap(y - k, YN)].astype(F32)
    lanes = lax.broadcasted_iota(jnp.int32, (32, 128), 1)
    masks = []
    for c in range(CAP):
        spot = lanes - 64 - 8 * c
        masks.append((lanes < 64) | ((spot >= 0) & (spot < length_of[c])))
    cross = jnp.concatenate(
        [jnp.where(masks[c], jnp.exp(total[32 * c : 32 * c + 32] * (HEAD_DIM**-0.5)), 0.0) for c in range(CAP)], axis=0
    )
    den = jnp.sum(cross, axis=1, keepdims=True)
    cwg[y] = cross.astype(BF16)
    sl = cwg.at[y]
    for k in FAR_FIRST:
        remote(sl, sl, sent.at[G_B], got.at[G_B], at_y(k)).start()
    load_v.wait()
    all_sent(G_A, cs.at[seven])
    all_got(G_B, cwg.at[seven])

    mixed = []
    for c in range(CAP):
        cw = jnp.concatenate([cwg[g, 32 * c : 32 * c + 32] for g in range(YN)], axis=0)
        mixed.append(jnp.dot(cw, ekeys[c], preferred_element_type=F32).astype(BF16))
    for g in range(YN):
        left = jnp.concatenate([mixed[c][32 * g : 32 * g + 32] for c in range(CAP)], axis=0)
        product = jnp.dot(left, dwv[:, 256 * g : 256 * g + 256], preferred_element_type=F32)
        rows = []
        for c in range(CAP):
            row = jnp.zeros((8, 256), F32)
            for h in range(4):
                low = 32 * c + 8 * h
                row += jnp.where(lane_head == h, product[low : low + 8], 0.0)
            rows.append(row)
        rows.append(jnp.zeros((8, 256), F32))
        ns[g] = jnp.concatenate(rows, axis=0).astype(BF16)
    scatter(ns, nr, G_N)
    all_sent(G_B, cwg.at[seven])
    all_got(G_N, nr.at[seven])
    num = ns[y].astype(F32)
    for k in range(1, 8):
        num += nr[wrap(y - k, YN)].astype(F32)

    lane = lax.broadcasted_iota(jnp.int32, (8, 128), 1)
    blocks = []
    for c in range(CAP):
        tail = jnp.where(lane == 4, asking[c].astype(F32), 0.0)
        for h in range(4):
            low = 32 * c + 8 * h
            tail = jnp.where(lane == h, den[low : low + 8], tail)
        blocks.append(jnp.concatenate([num[8 * c : 8 * c + 8], tail], axis=1))
    blocks.append(jnp.zeros((8, 384), F32))
    t1r[r8] = jnp.concatenate(blocks, axis=0).astype(BF16)
    sl = t1r.at[r8]
    for k in FAR_FIRST:
        remote(sl, sl, sent.at[G_F], got.at[G_F], at_xc(k)).start()
    all_sent(G_N, ns.at[seven])
    all_got(G_F, t1r.at[seven])
    sums = [jnp.zeros((8, 384), F32) for _ in range(ZN)]
    for source in range(8):
        from_there = t1r[source].astype(F32)
        for c in range(CAP):
            block = from_there[8 * c : 8 * c + 8]
            question = block[:, 260:261]
            for zz in range(ZN):
                here = question == (zz * 8 + r8).astype(F32)
                sums[zz] += jnp.where(here, block, 0.0)
    for zz in range(ZN):
        t2s[zz] = jnp.concatenate([sums[zz], jnp.zeros((8, 384), F32)], axis=0).astype(BF16)
    for k in FAR_FIRST:
        remote(t2s.at[wrap(z + k, ZN)], t2r.at[z], sent.at[G_H], got.at[G_H], at_z(k)).start()
    all_sent(G_F, t1r.at[seven])
    all_got(G_H, t2r.at[seven])
    answer = t2s[z].astype(F32)
    for k in range(1, 8):
        answer += t2r[wrap(z - k, ZN)].astype(F32)
    below = jnp.zeros((8, 256), F32)
    for h in range(4):
        below = jnp.where(lane_head == h, answer[0:8, 256 + h : 257 + h], below)
    out[0] = (answer[0:8, 0:256] / below).astype(BF16)
    all_sent(G_H, t2s.at[seven])


def body(
    question_states, passage_cache, norm_gain, enc_wq, enc_wk, enc_wv, enc_wo, dec_wk, dec_wv, dec_queries,
    passage_ids, location, question_lengths,
):
    vmem = pl.BlockSpec(memory_space=pltpu.VMEM)
    anywhere = pl.BlockSpec(memory_space=pl.ANY)
    dma = pltpu.SemaphoreType.DMA
    return pl.pallas_call(
        kernel,
        name="step",
        out_shape=jax.ShapeDtypeStruct((1, 8, 256), BF16),
        in_specs=[anywhere] * 13,
        out_specs=vmem,
        scratch_shapes=[
            pltpu.SMEM((2, 64), jnp.int32),
            pltpu.SMEM((256,), jnp.int32),
            pltpu.SMEM((64,), jnp.int32),
            pltpu.VMEM((1, 8, 512), BF16),
            pltpu.VMEM((4, 64, 512), BF16),
            pltpu.VMEM((32, 128), F32),
            pltpu.VMEM((1, 8, 256), BF16),
            pltpu.VMEM((64, 64, 768), BF16),
            pltpu.VMEM((64, 64, 256), BF16),
            pltpu.VMEM((64, 256), BF16),
            pltpu.VMEM((8, 224, 512), BF16),
            pltpu.VMEM((64, 16, 384), BF16),
            pltpu.VMEM((8, 32, 256), BF16),
            pltpu.VMEM((224, 4096), BF16),
            pltpu.VMEM((8, 2, 224, 128), BF16),
            pltpu.VMEM((224, 512), BF16),
            pltpu.VMEM((3, 128, 512), BF16),
            pltpu.VMEM((3, 256, 512), BF16),
            pltpu.VMEM((8, 96, 128), BF16),
            pltpu.VMEM((8, 96, 128), BF16),
            pltpu.VMEM((8, 96, 128), BF16),
            pltpu.VMEM((8, 32, 256), BF16),
            pltpu.VMEM((8, 32, 256), BF16),
            pltpu.VMEM((8, 32, 384), BF16),
            pltpu.VMEM((8, 16, 384), BF16),
            pltpu.VMEM((8, 16, 384), BF16),
            pltpu.VMEM((512, 2048), BF16),
            pltpu.VMEM((512, 2048), BF16),
            dma((13,)),
            dma((2, 5)),
            dma((8, 2, 5)),
            dma((1,)),
            dma((3, 2, 5)),
            dma((2, 10)),
            dma((17,)),
            dma((17,)),
        ],
        compiler_params=pltpu.CompilerParams(
            collective_id=0, has_side_effects=True, vmem_limit_bytes=56 * 2**20
        ),
    )(
        passage_ids.T, location, question_lengths, question_states, passage_cache, norm_gain.reshape(32, 128),
        enc_wq, enc_wk, enc_wv, enc_wo.T,
        dec_wk, dec_wv, dec_queries,
    )


def solution(mesh):
    in_specs = (
        P("mem", None, "dec"),
        P("mem", None, "dec"),
        P(),
        P("mem", "dec"),
        P("mem", "dec"),
        P("mem", "dec"),
        P("dec", "mem"),
        P("dec", None),
        P("dec", None),
        P("mem", None, "dec"),
        P(),
        P(),
        P(),
    )
    return jax.shard_map(body, mesh=mesh, in_specs=in_specs, out_specs=P("mem", None, "dec"), check_vma=False)
```

time: 103 us -> 98.7 us (0.958)
  Pallas kernels: 102 us -> 97.3 us
    pallas_call x1, Pallas kernels: 102 us -> 97.3 us  [body(): pl.pallas_call(kernel, name='step', out_shape=jax.ShapeDtypeStruct((1, 8,...]
where the time goes in v3:
time: 98.7 us; the launch traced here: 98.6 us
  Pallas kernels  97.3 us (99%)
  local copies, waits for them, and re-layouts  1.28 us (1%)
    pallas_call x1, Pallas kernels, body(): pl.pallas_call(kernel, name='step', out_shape=jax.ShapeDtypeStruct((1, 8,...  97.3 us

profile of v3, /device:TPU:1, one launch (start us, length us, event | category | flops | bytes accessed | tf_op | source)
XLA Modules:
  0.0 98.6 jit_solution(17841457378938825439)
XLA Ops:
  0.0 97.3 %step.1 = bf16[1,8,256]{2,1,0:T(8,128)(2,1)} custom-call(s32[2,64]{1,0:T(2,128)} %bitcast.5, s32[256]{0:T(256)} %rows_in.1, s32[64]{0:T(128)} %lengths_in.1, bf16[1,8,512]{2,1,0:T(8,128)(2,1)} %qs_in.1, bf16[4,64,512]{2,1,0:T(8,128)(2,1)} %cache_in.1, f32[32,128]{1,0:T(8,128)} %bitcast.4, bf16[64,256]{1,0:T(8,128)(2,1)} %wq_in.1, bf16[64,256]{1,0:T(8,128)(2,1)} %wk_in.1, ...), custom_call_target="tpu_custom_call" | custom-call | tf_op jit(solution)/shard_map/step/pallas_call | solution.py:578
  97.3 1.3 %copy.15 = bf16[1,8,256]{2,1,0:T(8,128)(2,1)} copy(bf16[1,8,256]{2,1,0:T(8,128)(2,1)} %step.1) | data formatting | bytes 8192

commit v4 on v3

--- a/solution.py
+++ b/solution.py
@@ -12,7 +12,7 @@
 ZN, XN, YN = 8, 4, 8
 CAP = 3
 MODES = (("hybrid", "ring"), ("direct", "ring"))
-(G_QZ, G_QX, G_QS, G_QY, G_DY, G_WP, G_WZ, G_WX, G_WS, G_CTX, G_A, G_B, G_N, G_F, G_H, G_RING, G_ROWS) = range(17)
+(G_QZ, G_QX, G_QS, G_QY, G_WP, G_WZ, G_WX, G_WS, G_CTX, G_A, G_B, G_N, G_F, G_H, G_RING, G_SIB, G_ROWS) = range(17)
 HEAD_DIM = 64
 NORM_EPSILON = 1e-06
 FAR_FIRST = (4, 3, 5, 2, 6, 1, 7)
@@ -31,7 +31,7 @@
     ids_in, rows_in, lengths_in, qs_in, cache_in, gain_in, wq_in, wk_in, wv_in, wo_in, dwk_in, dwv_in, dq_in,
     out,
     ids, rows_of, lengths, qs, cache, gain, dq,
-    wg, wot, wot_own, xg, qg, dqg, xn, ctxg, enc, ekeys, dqp, cs, cr, cwg, ns, nr, t1r, t2s, t2r, dwk, dwv,
+    wg, wot, wot_own, xg, qg, xn, ctxg, enc, ekeys, dqp, cs, cr, cwg, ns, nr, t1r, t2s, t2r, dwk, dwv,
     load_sem, ring1, ring2, sib_recv, rows_recv, ctx_sem, sent, got,
 ):
     m = lax.axis_index("mem")
@@ -88,9 +88,9 @@
             [
                 (ids_in, ids), (rows_in, rows_of), (lengths_in, lengths),
                 (cache_in, cache), (qs_in, qs), (dq_in, dq), (wo_in, wot_own), (gain_in, gain),
-                (wq_in, wg.at[m, :, pl.ds(0, 256)]),
-                (wk_in, wg.at[m, :, pl.ds(256, 256)]),
-                (wv_in, wg.at[m, :, pl.ds(512, 256)]),
+                (wq_in, wg.at[core, m // 2, :, pl.ds(0, 256)]),
+                (wk_in, wg.at[core, m // 2, :, pl.ds(256, 256)]),
+                (wv_in, wg.at[core, m // 2, :, pl.ds(512, 256)]),
                 (dwk_in, dwk), (dwv_in, dwv),
             ]
         )
@@ -151,10 +151,9 @@
         sl = qg.at[pl.ds(cc * (XN * ZN), XN * ZN)]
         return remote(sl, sl, sent.at[G_QS], got.at[G_QS], sibling)
 
-    def q_y(which, k, source):
-        sl = (dqg.at[wrap(source, YN)], xg.at[wrap(source, YN), pl.ds(192, 32)])[which]
-        group = (G_DY, G_QY)[which]
-        return remote(sl, sl, sent.at[group], got.at[group], at_y(k))
+    def q_y(k):
+        sl = xg.at[y, pl.ds(192, 48)]
+        return remote(sl, sl, sent.at[G_QY], got.at[G_QY], at_y(k))
 
     def question_0():
         for k in FAR_FIRST:
@@ -180,16 +179,13 @@
         rows.append(jnp.zeros((8, 512), F32))
         queries.append(jnp.zeros((8, 256), F32))
         xg[y, 192:224, :] = jnp.concatenate(rows, axis=0).astype(BF16)
-        dqg[y] = jnp.concatenate(queries, axis=0).astype(BF16)
-        for which in (1, 0):
-            for k in FAR_FIRST:
-                q_y(which, k, y).start()
-
-    def question_end(which):
-        if which:
-            all_got(G_QY, xg.at[0])
-        else:
-            all_got(G_DY, dqg.at[pl.ds(0, 7)])
+        both = [jnp.concatenate(queries[low : low + 2], axis=0) for low in (0, 2)]
+        xg[y, 224:240, :] = jnp.concatenate(both, axis=1).astype(BF16)
+        for k in FAR_FIRST:
+            q_y(k).start()
+
+    def question_end():
+        all_got(G_QY, xg.at[pl.ds(0, 7), pl.ds(192, 48)])
 
     def w_swap():
         return remote(wot_own, wot.at[(lax.rem(r8, 2) * XN + r8 // 2) * ZN + y], sent.at[G_WP], got.at[G_WP], swap)
@@ -228,26 +224,25 @@
         all_got(G_WX, wot.at[pl.ds(0, 24)])
         w_s(core).start()
 
-    def y_copy(c, sign, step, source):
+    def y_copy(sign, step, source):
         if step < YN // 2:
-            sl = xg.at[wrap(source, YN), pl.ds(64 * c, 64)]
+            sl = xg.at[wrap(source, YN), pl.ds(0, 192)]
         else:
-            sl = xg.at[wrap(source, YN), pl.ds(64 * c + (0 if sign > 0 else 32), 32)]
-        d = 0 if sign > 0 else 1
-        return remote(sl, sl, sent.at[G_ROWS], rows_recv.at[c, d, step], at_y(sign))
+            sl = xg.at[wrap(source, YN), pl.ds(0 if sign > 0 else 96, 96)]
+        return remote(sl, sl, sent.at[G_ROWS], rows_recv.at[0 if sign > 0 else 1, step], at_y(sign))
 
     def rows_step(step):
-        for c in range(CAP):
-            for sign in (1, -1):
-                if step > 0:
-                    y_copy(c, sign, step, y - sign * step).wait_recv()
-                if step < YN // 2:
-                    y_copy(c, sign, step + 1, y - sign * step).start()
+        for sign in (1, -1):
+            if step > 0:
+                y_copy(sign, step, y - sign * step).wait_recv()
+            if step < YN // 2:
+                y_copy(sign, step + 1, y - sign * step).start()
 
     def weights(role):
         n1, n2 = (ZN, XN) if role == 0 else (XN, ZN)
         i1, i2 = (z, x) if role == 0 else (x, z)
         mode_1, mode_2 = MODES[role]
+        landed = {}
 
         def away(dim, distance):
             return at_z(distance) if (dim == 1) == (role == 0) else at_x(distance)
@@ -257,12 +252,16 @@
             return a * XN + b if role == 0 else b * XN + a
 
         def copy(o, p, half, recv, to):
-            index = chip(o, p) * 2 + role
-            sl = wg.at[index] if half is None else wg.at[index, pl.ds(32 * half, 32)]
+            index = chip(o, p)
+            sl = wg.at[role, index] if half is None else wg.at[role, index, pl.ds(32 * half, 32)]
             return remote(sl, sl, sent.at[G_RING], recv, to)
 
         def hand_over(o, p):
-            copy(o, p, None, sib_recv.at[0], sibling).start()
+            far = (o if role == 0 else p) % ZN
+            landed[far] = landed.get(far, 0) + 1
+            if landed[far] == XN:
+                sl = wg.at[role, pl.ds(wrap(z + far, ZN) * XN, XN)]
+                remote(sl, sl, sent.at[G_SIB], sib_recv.at[0], sibling).start()
 
         def way(sign):
             return 0 if sign > 0 else 1
@@ -322,7 +321,7 @@
         spread(2, 0)
         hand_over(0, 0)
         rows_step(0)
-        after = {1: question_1, 2: question_2, 3: question_3, 4: wout_1}
+        after = {1: question_1, 2: question_2, 3: lambda: (question_3(), wout_1())}
         for time in range(1, max(4, events[-1][0]) + 1):
             now = [event for event in events if event[0] == time]
             for _, _, dim, step, o in now:
@@ -348,24 +347,27 @@
         def _():
             weights(role)
 
-    question_end(1)
+    wout_2()
+    question_end()
     squares = jnp.zeros((224, 128), F32)
     for d in range(YN):
-        block = xg[d].astype(F32)
+        block = xg[d, 0:224].astype(F32)
         block = block * block
         squares += block[:, 0:128] + block[:, 128:256] + block[:, 256:384] + block[:, 384:512]
     inverse = lax.rsqrt(jnp.sum(squares, axis=1, keepdims=True) * (1.0 / (512 * YN)) + NORM_EPSILON)
     for d in range(YN):
         scale = jnp.concatenate([gain[4 * d + part : 4 * d + part + 1, :] for part in range(4)], axis=1)
-        xn[:, 512 * d : 512 * d + 512] = (xg[d].astype(F32) * inverse * scale).astype(BF16)
-
-    remote(wg.at[pl.ds(0, 32)], wg.at[pl.ds(0, 32)], sent.at[G_RING], sib_recv.at[0], sibling).wait_recv()
-    wout_2()
+        xn[:, 512 * d : 512 * d + 512] = (xg[d, 0:224].astype(F32) * inverse * scale).astype(BF16)
+
+    remote(wg.at[0], wg.at[0], sent.at[G_RING], sib_recv.at[0], sibling).wait_recv()
+
+    def weight_of(low):
+        return jnp.concatenate(
+            [wg[cc, chip, :, low : low + 256] for chip in range(ZN * XN) for cc in range(2)], axis=0
+        )
+
     queries, keys, values = (
-        jnp.dot(
-            xn[...], wg[:, :, 256 * part : 256 * part + 256].reshape(4096, 256), preferred_element_type=F32
-        ).astype(BF16)
-        for part in range(3)
+        jnp.dot(xn[...], weight_of(256 * part), preferred_element_type=F32).astype(BF16) for part in range(3)
     )
 
     def pair_of(index):
@@ -420,10 +422,10 @@
         remote(sl, sl, sent.at[G_CTX], ctx_sem.at[part, slot], at_y(2 * sign)).start()
 
     load_k.wait()
-    question_end(0)
     lane_head = lax.broadcasted_iota(jnp.int32, (8, 256), 1) // 64
     for g in range(YN):
-        asked = dqg[g].astype(F32)
+        asked = xg[g, 224:240, :].astype(F32)
+        asked = jnp.concatenate([asked[:, 0:256], asked[:, 256:512]], axis=0)
         blocks = []
         for c in range(CAP):
             for h in range(4):
@@ -433,13 +435,13 @@
         for c in range(CAP):
             dqp[c, 32 * g : 32 * g + 32, :] = product[32 * c : 32 * c + 32]
 
-    all_sent(G_RING, wg.at[pl.ds(0, 63)])
-    all_sent(G_ROWS, xg.at[pl.ds(0, 6)])
+    all_sent(G_RING, wg.at[0, pl.ds(0, 31)])
+    all_sent(G_SIB, wg.at[0])
+    all_sent(G_ROWS, xg.at[pl.ds(0, 7), pl.ds(0, 192)])
     all_sent(G_QZ, qg.at[pl.ds(0, 7)])
     all_sent(G_QX, qg.at[pl.ds(0, 24)])
     all_sent(G_QS, qg.at[pl.ds(0, 32)])
-    all_sent(G_QY, xg.at[0])
-    all_sent(G_DY, dqg.at[pl.ds(0, 7)])
+    all_sent(G_QY, xg.at[pl.ds(0, 7), pl.ds(192, 48)])
     all_sent(G_WZ, wot.at[pl.ds(0, 7)])
 
     @pl.when(has_swap)
@@ -465,7 +467,7 @@
             [wot[((r % 2) * XN + r // 2) * ZN + d] for r in range(8)], axis=0
         )
         attended += dot_nt(context, weight)
-    enc[...] = (xg[y].astype(F32) + attended).astype(BF16)
+    enc[...] = (xg[y, 0:224].astype(F32) + attended).astype(BF16)
 
     for c in range(CAP):
         ekeys[c, 0:64, :] = enc[64 * c : 64 * c + 64, :]
@@ -589,12 +591,11 @@
             pltpu.VMEM((4, 64, 512), BF16),
             pltpu.VMEM((32, 128), F32),
             pltpu.VMEM((1, 8, 256), BF16),
-            pltpu.VMEM((64, 64, 768), BF16),
+            pltpu.VMEM((2, 32, 64, 768), BF16),
             pltpu.VMEM((64, 64, 256), BF16),
             pltpu.VMEM((64, 256), BF16),
-            pltpu.VMEM((8, 224, 512), BF16),
+            pltpu.VMEM((8, 240, 512), BF16),
             pltpu.VMEM((64, 16, 384), BF16),
-            pltpu.VMEM((8, 32, 256), BF16),
             pltpu.VMEM((224, 4096), BF16),
             pltpu.VMEM((8, 2, 224, 128), BF16),
             pltpu.VMEM((224, 512), BF16),
@@ -614,7 +615,7 @@
             dma((2, 5)),
             dma((8, 2, 5)),
             dma((1,)),
-            dma((3, 2, 5)),
+            dma((2, 5)),
             dma((2, 10)),
             dma((17,)),
             dma((17,)),

time: 98.7 us -> 98.2 us (level)
  no operation moved by 1% of the time
where the time goes in v4:
time: 98.2 us; the launch traced here: 98.1 us
  Pallas kernels  96.8 us (99%)
  local copies, waits for them, and re-layouts  1.28 us (1%)
    pallas_call x1, Pallas kernels, body(): pl.pallas_call(kernel, name='step', out_shape=jax.ShapeDtypeStruct((1, 8,...  96.8 us

profile of v4, /device:TPU:1, one launch (start us, length us, event | category | flops | bytes accessed | tf_op | source)
XLA Modules:
  0.0 98.1 jit_solution(13279022528671417050)
XLA Ops:
  0.0 96.8 %step.1 = bf16[1,8,256]{2,1,0:T(8,128)(2,1)} custom-call(s32[2,64]{1,0:T(2,128)} %bitcast.5, s32[256]{0:T(256)} %rows_in.1, s32[64]{0:T(128)} %lengths_in.1, bf16[1,8,512]{2,1,0:T(8,128)(2,1)} %qs_in.1, bf16[4,64,512]{2,1,0:T(8,128)(2,1)} %cache_in.1, f32[32,128]{1,0:T(8,128)} %bitcast.4, bf16[64,256]{1,0:T(8,128)(2,1)} %wq_in.1, bf16[64,256]{1,0:T(8,128)(2,1)} %wk_in.1, ...), custom_call_target="tpu_custom_call" | custom-call | tf_op jit(solution)/shard_map/step/pallas_call | solution.py:580
  96.8 1.3 %copy.15 = bf16[1,8,256]{2,1,0:T(8,128)(2,1)} copy(bf16[1,8,256]{2,1,0:T(8,128)(2,1)} %step.1) | data formatting | bytes 8192
